TPU v7x, 32 devices: a whole 2x2x4 slice. The times are simulated.
32 devices in a mesh: dp: 4 (over z), ctx: 8 (over y, x, core).
Axes of the slice: x: 2, y: 2, z: 4, core: 2. Of those that a mesh axis runs over, the one named last changes fastest.
Arguments:
- tokens: bfloat16 [4, 262144, 128], P('dp', 'ctx'), may hold values from -6 to 6
- cotangent: bfloat16 [4, 262144, 128], P('dp', 'ctx'), may hold values from -6 to 6
- w_gate_value: bfloat16 [128, 256], replicated, may hold values from -0.5 to 0.5
- w_first: bfloat16 [512, 512], replicated, may hold values from -0.25 to 0.25
- w_second: bfloat16 [512, 512], replicated, may hold values from -0.25 to 0.25
- w_up: bfloat16 [128, 256], replicated, may hold values from -0.5 to 0.5
- w_down: bfloat16 [256, 128], replicated, may hold values from -0.375 to 0.375
Outputs:
- output: bfloat16 [4, 262144, 128], P('dp', 'ctx')
- grad_tokens: bfloat16 [4, 262144, 128], P('dp', 'ctx')
- grad_gate_value: float32 [128, 256], replicated
- grad_first: float32 [512, 512], replicated
- grad_second: float32 [512, 512], replicated
- grad_up: float32 [128, 256], replicated
- grad_down: float32 [256, 128], replicated
All inputs are finite; a program needn't handle non-finite values.
Results may differ from a plain program's by a relative error of at most 0.014.
Values may be sent and summed in bfloat16 or wider, within the bound.
A program may use at most 256 MiB of HBM per device.

v0:
```python
import jax
import jax.numpy as jnp
from jax import lax
from jax.sharding import PartitionSpec as P


def silu_slope(pre):
    sigma = jax.nn.sigmoid(pre)
    return sigma * (1.0 + pre * (1.0 - sigma))


def body(tokens, cotangent, w_gate_value, w_first, w_second, w_up, w_down):
    f32 = jnp.float32
    bf16 = jnp.bfloat16
    seq_rows = tokens.shape[1]
    width = tokens.shape[2]
    block_size = w_first.shape[0]
    local_blocks = seq_rows // block_size
    seq_in = tokens[0]
    seq_cot = cotangent[0]
    projected = jnp.dot(seq_in, w_gate_value, preferred_element_type=f32)
    gate = jax.nn.sigmoid(projected[:, :width])
    values = projected[:, width:].astype(bf16)
    value_blocks = values.reshape(local_blocks, block_size, width)
    first = jnp.einsum("ijc,jk->ikc", value_blocks, w_first, preferred_element_type=f32).astype(
        bf16
    )
    first_mid = lax.all_to_all(first, "ctx", split_axis=1, concat_axis=0, tiled=True)
    mixed_mid = jnp.einsum("ikc,im->mkc", first_mid, w_second, preferred_element_type=f32).astype(
        bf16
    )
    mixed_blocks = lax.all_to_all(mixed_mid, "ctx", split_axis=0, concat_axis=1, tiled=True)
    mixed = mixed_blocks.reshape(seq_rows, width)
    hidden = (seq_in.astype(f32) + gate * mixed.astype(f32)).astype(bf16)
    pre = jnp.dot(hidden, w_up, preferred_element_type=f32)
    activated = jax.nn.silu(pre).astype(bf16)
    output = (hidden.astype(f32) + jnp.dot(activated, w_down, preferred_element_type=f32)).astype(
        bf16
    )
    grad_down = jnp.dot(activated.T, seq_cot, preferred_element_type=f32)
    d_act = (jnp.dot(seq_cot, w_down.T, preferred_element_type=f32) * silu_slope(pre)).astype(bf16)
    grad_up = jnp.dot(hidden.T, d_act, preferred_element_type=f32)
    d_hidden = (seq_cot.astype(f32) + jnp.dot(d_act, w_up.T, preferred_element_type=f32)).astype(
        bf16
    )
    d_mixed = (d_hidden.astype(f32) * gate).astype(bf16)
    d_gate = d_hidden.astype(f32) * mixed.astype(f32) * gate * (1.0 - gate)
    d_mixed_blocks = d_mixed.reshape(local_blocks, block_size, width)
    d_mixed_mid = lax.all_to_all(d_mixed_blocks, "ctx", split_axis=1, concat_axis=0, tiled=True)
    d_first_mid = jnp.einsum(
        "mkc,im->ikc", d_mixed_mid, w_second, preferred_element_type=f32
    ).astype(bf16)
    grad_second = jnp.einsum("ikc,mkc->im", first_mid, d_mixed_mid, preferred_element_type=f32)
    d_first = lax.all_to_all(d_first_mid, "ctx", split_axis=0, concat_axis=1, tiled=True)
    d_values = jnp.einsum("ikc,jk->ijc", d_first, w_first, preferred_element_type=f32).reshape(
        seq_rows, width
    )
    grad_first = jnp.einsum("ijc,ikc->jk", value_blocks, d_first, preferred_element_type=f32)
    d_projected = jnp.concatenate([d_gate, d_values], axis=1).astype(bf16)
    grad_gate_value = jnp.dot(seq_in.T, d_projected, preferred_element_type=f32)
    grad_tokens = (
        d_hidden.astype(f32) + jnp.dot(d_projected, w_gate_value.T, preferred_element_type=f32)
    ).astype(bf16)
    summed = lax.psum((grad_gate_value, grad_first, grad_second, grad_up, grad_down), ("dp", "ctx"))
    scale = float(seq_rows * lax.axis_size("ctx") * lax.axis_size("dp")) ** (-0.5)
    return (
        output[None],
        grad_tokens[None],
        summed[0] * scale,
        summed[1] * scale,
        summed[2] * scale,
        summed[3] * scale,
        summed[4] * scale,
    )


def solution(mesh):
    placed = (P("dp", "ctx", None), P("dp", "ctx", None), P(), P(), P(), P(), P())
    return jax.shard_map(
        body,
        mesh=mesh,
        in_specs=placed,
        out_specs=(P("dp", "ctx", None), P("dp", "ctx", None), P(), P(), P(), P(), P()),
        check_vma=False,
    )
```

profile of v0, /device:TPU:0, one launch (start us, length us, event | category | flops | bytes accessed | tf_op | source)
XLA Modules:
  0.0 916.0 jit_solution(5892044233215038924)
XLA Ops:
  7.2 19.0 %fusion.20 = f32[32768,256]{1,0:T(8,128)} fusion(bf16[128,256]{1,0:T(8,128)(2,1)} %param.9, bf16[1,32768,128]{2,1,0:T(8,128)(2,1)} %param.7), kind=kOutput, calls=%fused_computation.33 | convolution fusion | flops 2147483648 | bytes 42008576 | tf_op jit(solution)/shard_map/dot_general | solution.py:21
  26.2 6.4 slice.25
  35.9 6.8 convert_bitcast_fusion.4
  42.7 11.9 %copy.60 = bf16[64,512,128]{2,0,1:T(8,128)(2,1)} copy(bf16[64,512,128]{1,2,0:T(8,128)(2,1)} %convert_bitcast_fusion.4) | data formatting | bytes 16777216 | tf_op jit(solution)/shard_map/convert_element_type | solution.py:25
  54.6 100.6 %all_to_all.63 = bf16[64,512,128]{2,0,1:T(8,128)(2,1)} all-to-all(bf16[64,512,128]{2,0,1:T(8,128)(2,1)} %copy.60), channel_id=1, replica_groups=mesh['dp'=4,'ctx'=8] {'ctx'}, dimensions={1} | all-to-all | bytes 16777216 | tf_op jit(solution)/shard_map/all_to_all | solution.py:28
  155.2 12.2 %copy.62 = bf16[8,64,64,128]{3,2,1,0:T(8,128)(2,1)} copy(bf16[8,64,64,128]{3,1,2,0:T(8,128)(2,1)} %bitcast.101) | data formatting | bytes 16777216 | tf_op jit(solution)/shard_map/all_to_all | solution.py:28
  167.4 40.2 %convert_bitcast_fusion.3 = bf16[512,64,128]{0,2,1:T(8,128)(2,1)} fusion(bf16[512,64,128]{2,1,0:T(8,128)(2,1)} %bitcast.97, bf16[512,512]{1,0:T(8,128)(2,1)S(1)} %copy-done), kind=kOutput, calls=%fused_computation.37 | convolution fusion | flops 4299161600 | bytes 17301504 | tf_op jit(solution)/shard_map/ikc,im->mkc/dot_general | solution.py:29
  207.6 12.0 %copy.64 = bf16[512,64,128]{2,1,0:T(8,128)(2,1)} copy(bf16[512,64,128]{0,2,1:T(8,128)(2,1)} %convert_bitcast_fusion.3) | data formatting | bytes 16777216 | tf_op jit(solution)/shard_map/convert_element_type | solution.py:29
  219.6 99.7 %all_to_all.64 = bf16[512,64,128]{2,1,0:T(8,128)(2,1)} all-to-all(bf16[512,64,128]{2,1,0:T(8,128)(2,1)} %copy.64), channel_id=1, replica_groups=mesh['dp'=4,'ctx'=8] {'ctx'}, dimensions={0} | all-to-all | bytes 16777216 | tf_op jit(solution)/shard_map/all_to_all | solution.py:32
  319.3 11.4 %convert_bitcast_fusion = f32[64,8,64,128]{3,2,0,1:T(8,128)} fusion(bf16[8,64,64,128]{3,2,1,0:T(8,128)(2,1)} %bitcast.94), kind=kLoop, calls=%fused_computation.19 | loop fusion | flops 4194304 | bytes 25165824 | tf_op jit(solution)/shard_map/convert_element_type | solution.py:34
  330.7 7.3 copy.65
  343.7 11.0 %fusion.11 = bf16[32768,128]{1,0:T(8,128)(2,1)} fusion(f32[64,8,64,128]{3,2,1,0:T(8,128)S(1)} %copy.65, bf16[1,32768,128]{2,1,0:T(8,128)(2,1)S(1)} %bitcast.91, f32[32768,256]{1,0:T(8,128)} %fusion.20), kind=kLoop, calls=%fused_computation.23 | loop fusion | flops 29360128 | bytes 50331648 | tf_op jit(solution)/shard_map/convert_element_type | solution.py:34
  354.7 23.7 %multiply_convert_fusion = (bf16[32768,256]{1,0:T(8,128)(2,1)}, f32[32768,256]{1,0:T(8,128)}) fusion(bf16[32768,128]{1,0:T(8,128)(2,1)} %fusion.11, bf16[128,256]{1,0:T(8,128)(2,1)S(1)} %copy-done.7), kind=kOutput, calls=%fused_computation.11 | convolution fusion | flops 2189426688 | bytes 58785792 | tf_op jit(solution)/shard_map/dot_general | solution.py:35
  378.4 24.8 %fusion = bf16[32768,256]{1,0:T(8,128)(2,1)} fusion(bf16[256,128]{1,0:T(8,128)(2,1)S(1)} %copy-done.6, f32[32768,256]{1,0:T(8,128)} %get-tuple-element.43, bf16[1,32768,128]{2,1,0:T(8,128)(2,1)} %param.8), kind=kOutput, calls=%fused_computation.1 | convolution fusion | flops 2222981120 | bytes 58785792 | tf_op jit(solution)/shard_map/dot_general | solution.py:41
  403.2 32.0 %fusion.14 = (bf16[32768,128]{1,0:T(8,128)(2,1)}, bf16[32768,128]{1,0:T(8,128)(2,1)}, f32[32768,128]{1,0:T(8,128)}) fusion(f32[64,8,64,128]{3,2,1,0:T(8,128)} %copy-done.1, f32[32768,256]{1,0:T(8,128)} %fusion.20, bf16[32768,256]{1,0:T(8,128)(2,1)} %fusion, bf16[128,256]{1,0:T(8,128)(2,1)S(1)} %copy-done.7, bf16[1,32768,128]{2,1,0:T(8,128)(2,1)} %param.8), kind=kOutput, calls=%fused_computation.26 | convolution fusion | flops 2206203904 | bytes 92340224 | tf_op jit(solution)/shard_map/dot_general | solution.py:43
  435.2 12.1 %copy.66 = bf16[64,512,128]{2,0,1:T(8,128)(2,1)} copy(bf16[64,512,128]{2,1,0:T(8,128)(2,1)} %bitcast.105) | data formatting | bytes 16777216 | tf_op jit(solution)/shard_map/reshape | solution.py:48
  447.3 99.7 %all_to_all.65 = bf16[64,512,128]{2,0,1:T(8,128)(2,1)} all-to-all(bf16[64,512,128]{2,0,1:T(8,128)(2,1)} %copy.66), channel_id=1, replica_groups=mesh['dp'=4,'ctx'=8] {'ctx'}, dimensions={1} | all-to-all | bytes 16777216 | tf_op jit(solution)/shard_map/all_to_all | solution.py:49
  547.0 12.0 %copy.68 = bf16[8,64,64,128]{3,2,1,0:T(8,128)(2,1)} copy(bf16[8,64,64,128]{3,1,2,0:T(8,128)(2,1)} %bitcast.102) | data formatting | bytes 16777216 | tf_op jit(solution)/shard_map/all_to_all | solution.py:49
  559.0 40.2 %convert_bitcast_fusion.2 = bf16[512,64,128]{0,2,1:T(8,128)(2,1)} fusion(bf16[512,64,128]{2,1,0:T(8,128)(2,1)} %bitcast.103, bf16[512,512]{1,0:T(8,128)(2,1)S(1)} %copy-done), kind=kOutput, calls=%fused_computation.36 | convolution fusion | flops 4299161600 | bytes 17301504 | tf_op jit(solution)/shard_map/mkc,im->ikc/dot_general | solution.py:50
  599.3 12.1 %copy.70 = bf16[512,64,128]{2,1,0:T(8,128)(2,1)} copy(bf16[512,64,128]{0,2,1:T(8,128)(2,1)} %convert_bitcast_fusion.2) | data formatting | bytes 16777216 | tf_op jit(solution)/shard_map/convert_element_type | solution.py:52
  616.4 15.4 %fusion.47 = f32[128,256]{0,1:T(8,128)} fusion(bf16[32768,128]{1,0:T(8,128)(2,1)} %fusion.11, bf16[32768,256]{1,0:T(8,128)(2,1)} %fusion), kind=kOutput, calls=%fused_computation.60 | convolution fusion | flops 2147483648 | bytes 25296896 | tf_op jit(solution)/shard_map/dot_general | solution.py:42
  631.8 13.5 %fusion.16 = f32[256,128]{1,0:T(8,128)} fusion(bf16[32768,256]{1,0:T(8,128)(2,1)} %get-tuple-element.42, bf16[1,32768,128]{2,1,0:T(8,128)(2,1)} %param.8), kind=kOutput, calls=%fused_computation.29 | convolution fusion | flops 2147483648 | bytes 25296896 | tf_op jit(solution)/shard_map/dot_general | solution.py:40
  645.3 13.6 %fusion.33 = f32[512,512]{1,0:T(8,128)} fusion(bf16[512,64,128]{2,1,0:T(8,128)(2,1)} %bitcast.104, bf16[512,64,128]{2,1,0:T(8,128)(2,1)S(1)} %bitcast.100), kind=kOutput, calls=%fused_computation.46 | convolution fusion | flops 4294967296 | bytes 17825792 | tf_op jit(solution)/shard_map/ikc,mkc->im/dot_general | solution.py:53
  658.9 51.5 %all-to-all-done.3 = bf16[512,64,128]{2,1,0:T(8,128)(2,1)} async-done(((bf16[512,64,128]{2,1,0:T(8,128)(2,1)}), bf16[512,64,128]{2,1,0:T(8,128)(2,1)}, u32[]{:S(2)}, u32[]{:S(2)}) %all-to-all-start.3) | async-done | bytes 8388640 | tf_op jit(solution)/shard_map/all_to_all | solution.py:54
  710.4 9.8 %copy.71 = bf16[64,8,64,128]{3,2,1,0:T(8,128)(2,1)} copy(bf16[64,8,64,128]{3,2,0,1:T(8,128)(2,1)} %bitcast.22) | data formatting | bytes 16777216 | tf_op jit(solution)/shard_map/all_to_all | solution.py:54
  720.2 11.4 %convolution_bitcast_fusion = f32[512,512]{1,0:T(8,128)} fusion(bf16[64,512,128]{2,1,0:T(8,128)(2,1)} %bitcast.96, bf16[64,512,128]{2,1,0:T(8,128)(2,1)} %bitcast.106), kind=kOutput, calls=%fused_computation.47 | convolution fusion | flops 4294967296 | bytes 17825792 | tf_op jit(solution)/shard_map/ijc,ikc->jk/dot_general | solution.py:58
  731.6 6.9 convert_bitcast_fusion.1
  738.5 12.1 %copy.73 = bf16[64,512,128]{2,1,0:T(8,128)(2,1)} copy(bf16[64,512,128]{1,2,0:T(8,128)(2,1)} %convert_bitcast_fusion.1) | data formatting | bytes 16777216 | tf_op jit(solution)/shard_map/ikc,jk->ijc/transpose | solution.py:55
  750.6 13.4 %fusion.38 = f32[128,256]{0,1:T(8,128)} fusion(bf16[1,32768,128]{2,1,0:T(8,128)(2,1)} %param.7, bf16[32768,128]{1,0:T(8,128)(2,1)} %bitcast.92, bf16[32768,128]{1,0:T(8,128)(2,1)} %get-tuple-element.40), kind=kOutput, calls=%fused_computation.48 | convolution fusion | flops 2181038080 | bytes 25296896 | tf_op jit(solution)/shard_map/dot_general | solution.py:60
  764.0 16.5 %fusion.6 = bf16[1,32768,128]{2,1,0:T(8,128)(2,1)} fusion(bf16[32768,256]{1,0:T(8,128)(2,1)} %get-tuple-element.42, bf16[256,128]{1,0:T(8,128)(2,1)S(1)} %copy-done.6, bf16[32768,128]{1,0:T(8,128)(2,1)} %fusion.11), kind=kOutput, calls=%fused_computation.10 | convolution fusion | flops 2160066560 | bytes 33619968 | tf_op jit(solution)/shard_map/dot_general | solution.py:37
  780.5 16.8 %fusion.5 = bf16[1,32768,128]{2,1,0:T(8,128)(2,1)} fusion(f32[32768,128]{1,0:T(8,128)} %get-tuple-element.44, bf16[128,256]{1,0:T(8,128)(2,1)S(1)} %copy-done.5, bf16[32768,128]{1,0:T(8,128)(2,1)} %bitcast.93, bf16[32768,128]{1,0:T(8,128)(2,1)} %get-tuple-element.40), kind=kOutput, calls=%fused_computation.9 | convolution fusion | flops 2189426688 | bytes 42008576 | tf_op jit(solution)/shard_map/dot_general | solution.py:62
  797.3 104.5 %all-reduce.3.cloned.1.call-done = (f32[128,256]{0,1:T(8,128)}, f32[512,512]{1,0:T(8,128)}, f32[512,512]{1,0:T(8,128)}, f32[128,256]{0,1:T(8,128)}, f32[256,128]{1,0:T(8,128)}) async-done(((f32[128,256]{0,1:T(8,128)}, f32[512,512]{1,0:T(8,128)}, f32[512,512]{1,0:T(8,128)}, f32[128,256]{0,1:T(8,128)}, f32[256,128]{1,0:T(8,128)}), (f32[128,256]{0,1:T(8,128)}, f32[512,512]{1,0:T(8,128)}, f32[512,512]{1,0:T(8,128)}, ...) | async-done | bytes 2490384 | tf_op jit(solution)/shard_map/psum | solution.py:64
  (39 shorter events, 21.2 us)
Async XLA Ops:
  7.2 160.2 %copy-start = (bf16[512,512]{1,0:T(8,128)(2,1)S(1)}, bf16[512,512]{1,0:T(8,128)(2,1)}, u32[]{:S(2)}) copy-start(bf16[512,512]{1,0:T(8,128)(2,1)} %param.11) | copy-start | bytes 1572868
  26.2 9.7 %copy-start.3 = (bf16[512,512]{1,0:T(8,128)(2,1)S(1)}, bf16[512,512]{1,0:T(8,128)(2,1)}, u32[]{:S(2)}) copy-start(bf16[512,512]{1,0:T(8,128)(2,1)} %param.10) | copy-start | bytes 1572868
  32.6 3.3 copy-start.2
  319.3 24.4 %slice-start = ((s8[8388608]{0:T(1024)(128)(4,1)}), s8[4194304]{0:T(1024)(128)(4,1)S(1)}, s32[]{:S(2)}) async-start(s8[8388608]{0:T(1024)(128)(4,1)} %bitcast.90), calls=%async_computation.5 | async-start | bytes 8388608
  330.7 13.0 %slice-start.1 = ((s8[8388608]{0:T(1024)(128)(4,1)}), s8[4194304]{0:T(1024)(128)(4,1)S(1)}, s32[]{:S(2)}) async-start(s8[8388608]{0:T(1024)(128)(4,1)} %bitcast.90), calls=%async_computation.6 | async-start | bytes 8388608
  338.0 5.7 copy-start.1
  343.7 11.0 %copy-start.7 = (bf16[128,256]{1,0:T(8,128)(2,1)S(1)}, bf16[128,256]{1,0:T(8,128)(2,1)}, u32[]{:S(2)}) copy-start(bf16[128,256]{1,0:T(8,128)(2,1)} %param.12) | copy-start | bytes 196612
  354.7 23.7 %copy-start.6 = (bf16[256,128]{1,0:T(8,128)(2,1)S(1)}, bf16[256,128]{1,0:T(8,128)(2,1)}, u32[]{:S(2)}) copy-start(bf16[256,128]{1,0:T(8,128)(2,1)} %param.13) | copy-start | bytes 196612
  611.3 99.0 %all-to-all-start.3 = ((bf16[512,64,128]{2,1,0:T(8,128)(2,1)}), bf16[512,64,128]{2,1,0:T(8,128)(2,1)}, u32[]{:S(2)}, u32[]{:S(2)}) async-start(bf16[512,64,128]{2,1,0:T(8,128)(2,1)} %copy.70), calls=%async_computation.3 | async-start | bytes 16777216 | tf_op jit(solution)/shard_map/all_to_all | solution.py:54
  616.3 285.5 %all-reduce.3.cloned.1.call-start = ((), (), s32[]{:S(2)}) async-start(), calls=%async_computation.4 | async-start | bytes 4980736 | tf_op jit(solution)/shard_map/psum | solution.py:64
  631.8 13.5 %slice-start.2 = ((s8[8388608]{0:T(1024)(128)(4,1)}), s8[4194304]{0:T(1024)(128)(4,1)S(1)}, s32[]{:S(2)}) async-start(s8[8388608]{0:T(1024)(128)(4,1)} %bitcast.98), calls=%async_computation.7 | async-start | bytes 8388608
  631.8 13.5 %slice-start.3 = ((s8[8388608]{0:T(1024)(128)(4,1)}), s8[4194304]{0:T(1024)(128)(4,1)S(1)}, s32[]{:S(2)}) async-start(s8[8388608]{0:T(1024)(128)(4,1)} %bitcast.98), calls=%async_computation.8 | async-start | bytes 8388608
  720.2 11.4 %slice-start.4 = ((s8[8388608]{0:T(1024)(128)(4,1)}), s8[4194304]{0:T(1024)(128)(4,1)S(1)}, s32[]{:S(2)}) async-start(s8[8388608]{0:T(1024)(128)(4,1)} %bitcast.107), calls=%async_computation.9 | async-start | bytes 8388608
  720.2 11.4 %copy-start.4 = (bf16[512,512]{1,0:T(8,128)(2,1)S(1)}, bf16[512,512]{1,0:T(8,128)(2,1)}, u32[]{:S(2)}) copy-start(bf16[512,512]{1,0:T(8,128)(2,1)} %param.10) | copy-start | bytes 1572868
  720.2 11.4 %slice-start.5 = ((s8[8388608]{0:T(1024)(128)(4,1)}), s8[4194304]{0:T(1024)(128)(4,1)S(1)}, s32[]{:S(2)}) async-start(s8[8388608]{0:T(1024)(128)(4,1)} %bitcast.107), calls=%async_computation.10 | async-start | bytes 8388608
  764.0 16.5 %copy-start.5 = (bf16[128,256]{1,0:T(8,128)(2,1)S(1)}, bf16[128,256]{1,0:T(8,128)(2,1)}, u32[]{:S(2)}) copy-start(bf16[128,256]{1,0:T(8,128)(2,1)} %param.9) | copy-start | bytes 196612
Sparse Core Ops, SparseCore 0:
  764.1 137.6 all-reduce.2
where the time goes:
time: 923 us; the launch traced here: 916 us
  blocking collectives  300 us (33%)
  matrix products  294 us (32%)
  waiting for transfers between devices  156 us (17%)
  local copies, waits for them, and re-layouts  118 us (13%)
  other arithmetic  28 us (3%)
  between operations  14.4 us (2%)
    psum x1, waiting for transfers between devices, body(): lax.psum((grad_gate_value, grad_first, grad_second, grad_up, grad_down),...  104 us
    all_to_all x1, blocking collectives, body(): lax.all_to_all(first, 'ctx', split_axis=1, concat_axis=0, tiled=True)  101 us
    all_to_all x1, blocking collectives, body(): lax.all_to_all(mixed_mid, 'ctx', split_axis=0, concat_axis=1, tiled=True)  99.7 us
    all_to_all x1, blocking collectives, body(): lax.all_to_all(d_mixed_blocks, 'ctx', split_axis=1, concat_axis=0, tiled=...  99.7 us
    all_to_all x1, waiting for transfers between devices, body(): lax.all_to_all(d_first_mid, 'ctx', split_axis=0, concat_axis=1, tiled=True)  51.5 us
    dot_general x1, matrix products, body(): jnp.einsum('mkc,im->ikc', d_mixed_mid, w_second, preferred_element_type=f32)  40.2 us
    dot_general x1, matrix products, body(): jnp.einsum('ikc,im->mkc', first_mid, w_second, preferred_element_type=f32)  40.2 us
    dot_general x1, matrix products, body(): jnp.dot(d_act, w_up.T, preferred_element_type=f32)  32 us
  transfers between devices with their start and end apart: 2, of which 2 were waited for; matrix products, arithmetic and copies ran while one was open for 8% of the time, Pallas kernels for 0%

commit v1 on v0

v1 whole, which is shorter than its diff:
```python
import functools

import jax
import jax.numpy as jnp
from jax import lax
from jax.experimental import pallas as pl
from jax.experimental.pallas import tpu as pltpu
from jax.sharding import PartitionSpec as P

F32 = jnp.float32
BF16 = jnp.bfloat16
TILE = 16
VMEM_LIMIT = 56 * 1024 * 1024


def sig(v):
    return 0.5 * jnp.tanh(0.5 * v) + 0.5


def dot(a, b):
    return jnp.dot(a, b, preferred_element_type=F32)


def dot_rows(a, b):
    return lax.dot_general(a, b, (((0,), (0,)), ((), ())), preferred_element_type=F32)


def dot_lanes(a, b):
    return lax.dot_general(a, b, (((1,), (1,)), ((), ())), preferred_element_type=F32)


def lanes(ref, count):
    return jnp.concatenate([ref[b] for b in range(count)], axis=1)


def params():
    return pltpu.CompilerParams(vmem_limit_bytes=VMEM_LIMIT)


def cost(flops, nbytes, trans=0):
    return pl.CostEstimate(flops=int(flops), bytes_accessed=int(nbytes), transcendentals=int(trans))


def whole(array):
    zeros = (0,) * array.ndim
    return pl.BlockSpec(array.shape, lambda *_: zeros)


def first_kernel(from_tokens, *refs):
    if from_tokens:
        src, wv, w1t, val, *outs = refs
        rows = src.shape[0] * src.shape[1]
        val[...] = dot(src[...].reshape(rows, src.shape[2]), wv[...]).astype(BF16).reshape(val.shape)
    else:
        val, w1t, *outs = refs
    width = val.shape[2]
    vals = lanes(val, TILE)
    per = outs[0].shape[0]
    for at, out in enumerate(outs):
        res = dot(w1t[at * per : (at + 1) * per, :], vals)
        parts = jnp.stack([res[:, b * width : (b + 1) * width] for b in range(TILE)], 0)
        out[...] = jnp.swapaxes(parts, 0, 1).astype(BF16)


def first_call(src, wv, w1t, per):
    blocks, steps, width = src.shape
    outs = w1t.shape[0] // per
    tile = pl.BlockSpec((TILE, steps, width), lambda t: (t, 0, 0))
    sent = pl.BlockSpec((per, TILE, width), lambda t: (0, t, 0))
    sent_shape = jax.ShapeDtypeStruct((per, blocks, width), BF16)
    flops = 2 * blocks * steps * width * w1t.shape[0]
    if wv is not None:
        return pl.pallas_call(
            functools.partial(first_kernel, True),
            grid=(blocks // TILE,),
            in_specs=[tile, whole(wv), whole(w1t)],
            out_specs=[tile] + [sent] * outs,
            out_shape=[jax.ShapeDtypeStruct(src.shape, BF16)] + [sent_shape] * outs,
            compiler_params=params(),
            cost_estimate=cost(flops + 2 * src.size * width, 4 * src.size + 2 * per * blocks * width),
            name="values_first",
        )(src, wv, w1t)
    return pl.pallas_call(
        functools.partial(first_kernel, False),
        grid=(blocks // TILE,),
        in_specs=[tile, whole(w1t)],
        out_specs=[sent] * outs,
        out_shape=[sent_shape] * outs,
        compiler_params=params(),
        cost_estimate=cost(flops, 2 * src.size + 2 * outs * per * blocks * width),
        name="first_rest",
    )(src, w1t)


def gather_positions(ref, count, order, width):
    return jnp.concatenate([ref[:, q].reshape(order, width) for q in range(count)], axis=1)


def spread_positions(ref, res, count, width):
    n, _, rows, _ = ref.shape
    for q in range(count):
        ref[:, q] = res[:, q * width : (q + 1) * width].astype(BF16).reshape(n, rows, width)


def mix_kernel(x, w, out):
    n, count, rows, width = x.shape
    spread_positions(out, dot(w[...], gather_positions(x, count, n * rows, width)), count, width)


def mix_back_kernel(x, d, w, out, grad):
    n, count, rows, width = x.shape

    @pl.when(pl.program_id(0) == 0)
    def _():
        grad[...] = jnp.zeros_like(grad)

    dm = gather_positions(d, count, n * rows, width)
    spread_positions(out, dot(w[...], dm), count, width)
    grad[...] += dot_lanes(gather_positions(x, count, n * rows, width), dm)


def mix_call(x, w):
    n, per, rows, width = x.shape
    count = min(4, per)
    spec = pl.BlockSpec((n, count, rows, width), lambda t: (0, t, 0, 0))
    return pl.pallas_call(
        mix_kernel,
        grid=(per // count,),
        in_specs=[spec, whole(w)],
        out_specs=spec,
        out_shape=jax.ShapeDtypeStruct(x.shape, BF16),
        compiler_params=params(),
        cost_estimate=cost(2 * x.size * w.shape[0], 4 * x.size),
        name="mix",
    )(x, w)


def mix_back_call(x, d, w):
    n, per, rows, width = x.shape
    count = min(4, per)
    spec = pl.BlockSpec((n, count, rows, width), lambda t: (0, t, 0, 0))
    return pl.pallas_call(
        mix_back_kernel,
        grid=(per // count,),
        in_specs=[spec, spec, whole(w)],
        out_specs=[spec, whole(w)],
        out_shape=[jax.ShapeDtypeStruct(x.shape, BF16), jax.ShapeDtypeStruct(w.shape, F32)],
        compiler_params=params(),
        cost_estimate=cost(4 * x.size * w.shape[0], 6 * x.size),
        name="mix_back",
    )(x, d, w)


def mlp_kernel(tok, cot, mix, wg, wgt, wu, wut, wd, wdt, *rest):
    out, part, dmix, gdown, gup, ggate, mixed, dback = rest[-8:]
    width = tok.shape[2]
    steps = tok.shape[1]
    sub = 4

    @pl.when(pl.program_id(0) == 0)
    def _():
        gdown[...] = jnp.zeros_like(gdown)
        gup[...] = jnp.zeros_like(gup)
        ggate[...] = jnp.zeros_like(ggate)

    mixed[...] = jnp.swapaxes(mix[...].astype(F32), 0, 1)

    @pl.loop(0, TILE // sub)
    def _(s):
        at = pl.ds(s * sub, sub)
        flat = (sub * steps, width)
        back = (sub, steps, width)
        t = tok[at].reshape(flat)
        ct = cot[at].reshape(flat)
        m = mixed[at].reshape(flat)
        gate = sig(dot(t, wg[...]))
        hidden = (t.astype(F32) + gate * m).astype(BF16)
        pre = dot(hidden, wu[...])
        sg = sig(pre)
        act = (pre * sg).astype(BF16)
        out[at] = (hidden.astype(F32) + dot(act, wd[...])).astype(BF16).reshape(back)
        dact = (dot(ct, wdt[...]) * (sg * (1.0 + pre * (1.0 - sg)))).astype(BF16)
        gdown[...] += dot_rows(act, ct)
        gup[...] += dot_rows(hidden, dact)
        dh = (ct.astype(F32) + dot(dact, wut[...])).astype(BF16).astype(F32)
        dm = dh * gate
        dback[at] = dm.reshape(back)
        dgate = (dm * m * (1.0 - gate)).astype(BF16)
        part[at] = (dh + dot(dgate, wgt[...])).astype(BF16).reshape(back)
        ggate[...] += dot_rows(t, dgate)

    dmix[...] = jnp.swapaxes(dback[...], 0, 1).astype(BF16)


def mlp_call(chunk, tokens, cot, mix, weights, carried):
    blocks, steps, width = tokens.shape
    per = mix.shape[0]
    wg, wgt, wu, wut, wd, wdt = weights
    tile = pl.BlockSpec((TILE, per, width), lambda t: (t, chunk, 0))
    mid = pl.BlockSpec((per, TILE, width), lambda t: (0, t, 0))
    held = [pl.BlockSpec(memory_space=pl.ANY)] * len(carried)
    grads = [wd, wu, wg]
    rows = blocks * per
    full = jax.ShapeDtypeStruct(tokens.shape, BF16)
    return pl.pallas_call(
        mlp_kernel,
        grid=(blocks // TILE,),
        in_specs=[tile, tile, mid] + [whole(w) for w in weights] + held,
        out_specs=[tile, tile, mid] + [whole(g) for g in grads],
        out_shape=[full, full, jax.ShapeDtypeStruct(mix.shape, BF16)]
        + [jax.ShapeDtypeStruct(g.shape, F32) for g in grads],
        scratch_shapes=[pltpu.VMEM((TILE, per, width), F32)] * 2,
        input_output_aliases={9 + a: a for a in range(len(carried))},
        compiler_params=params(),
        cost_estimate=cost(2 * rows * (6 * wu.size + 3 * wg.size), 12 * rows * width, rows * 3 * width),
        name="mlp",
    )(tokens, cot, mix, *weights, *carried)


def back_kernel(d, val, *rest):
    out, grad = rest[-2:]

    @pl.when(pl.program_id(0) == 0)
    def _():
        grad[...] = jnp.zeros_like(grad)

    out[...] = jnp.swapaxes(d[...].astype(F32), 0, 1).astype(BF16)
    grad[...] += dot_lanes(lanes(val, TILE), lanes(out, TILE))


def back_call(chunk, d, values, carried):
    blocks, steps, width = values.shape
    per = d.shape[0]
    held = [pl.BlockSpec(memory_space=pl.ANY)] * len(carried)
    return pl.pallas_call(
        back_kernel,
        grid=(blocks // TILE,),
        in_specs=[
            pl.BlockSpec((per, TILE, width), lambda t: (0, t, 0)),
            pl.BlockSpec((TILE, steps, width), lambda t: (t, 0, 0)),
        ]
        + held,
        out_specs=[
            pl.BlockSpec((TILE, per, width), lambda t: (t, chunk, 0)),
            pl.BlockSpec((steps, per), lambda t: (0, 0)),
        ],
        out_shape=[
            jax.ShapeDtypeStruct(values.shape, BF16),
            jax.ShapeDtypeStruct((steps, per), F32),
        ],
        input_output_aliases={2 + a: a for a in range(len(carried))},
        compiler_params=params(),
        cost_estimate=cost(2 * values.size * per, 2 * values.size + 4 * d.size),
        name="first_back",
    )(d, values, *carried)


def tokens_kernel(d, part, tok, w1, wvt, out, grad):
    width = tok.shape[2]

    @pl.when(pl.program_id(0) == 0)
    def _():
        grad[...] = jnp.zeros_like(grad)

    res = dot(w1[...], lanes(d, TILE))
    total = grad[...]
    for b in range(TILE):
        dv = res[:, b * width : (b + 1) * width].astype(BF16)
        out[b] = (part[b].astype(F32) + dot(dv, wvt[...])).astype(BF16)
        total += dot_rows(tok[b], dv)
    grad[...] = total


def tokens_call(d, part, tokens, w1, wvt):
    blocks, steps, width = tokens.shape
    tile = pl.BlockSpec((TILE, steps, width), lambda t: (t, 0, 0))
    return pl.pallas_call(
        tokens_kernel,
        grid=(blocks // TILE,),
        in_specs=[tile, tile, tile, whole(w1), whole(wvt)],
        out_specs=[tile, whole(wvt)],
        out_shape=[jax.ShapeDtypeStruct(tokens.shape, BF16), jax.ShapeDtypeStruct(wvt.shape, F32)],
        compiler_params=params(),
        cost_estimate=cost(2 * tokens.size * (steps + 2 * width), 8 * tokens.size),
        name="grad_tokens",
    )(d, part, tokens, w1, wvt)


def body(tokens, cotangent, w_gate_value, w_first, w_second, w_up, w_down):
    n = lax.axis_size("ctx")
    seq_rows, width = tokens.shape[1:]
    steps = w_first.shape[0]
    blocks = seq_rows // steps
    chunks = 4
    per = steps // chunks
    tok = tokens.reshape(blocks, steps, width)
    cot = cotangent.reshape(blocks, steps, width)
    wg, wv = w_gate_value[:, :width], w_gate_value[:, width:]
    w1t = w_first.T
    w2t = w_second.T
    weights = (wg, wg.T, w_up, w_up.T, w_down, w_down.T)

    def exchange(a):
        moved = lax.all_to_all(
            a.reshape(n, per // n, blocks, width), "ctx", split_axis=0, concat_axis=0, tiled=True
        )
        return moved

    values, lead = first_call(tok, wv, w1t[:per], per)
    firsts = [lead, *first_call(values, None, w1t[per:], per)]

    first_mid, mixed, d_mixed, d_first = {}, {}, {}, {}
    small, second, first_cols = [], [], []
    carried, carried_d = (), ()
    for at in range(chunks + 3):
        if at < chunks:
            first_mid[at] = exchange(firsts[at])
        c = at - 1
        if 0 <= c < chunks:
            mixed[c] = exchange(mix_call(first_mid[c], w2t)).reshape(per, blocks, width)
        c = at - 2
        if 0 <= c < chunks:
            out, part, dm, *grads = mlp_call(c, tok, cot, mixed[c], weights, carried)
            carried = (out, part)
            small.append(grads)
            d_mixed[c] = exchange(dm)
        c = at - 3
        if 0 <= c < chunks:
            df, g2 = mix_back_call(first_mid[c], d_mixed[c], w_second)
            second.append(g2)
            d_first[c] = exchange(df).reshape(per, blocks, width)
    for c in range(chunks):
        filled, cols = back_call(c, d_first[c], values, carried_d)
        carried_d = (filled,)
        first_cols.append(cols)
    grad_down, grad_up, grad_gate = [sum(parts) for parts in zip(*small)]
    grad_tokens, grad_value = tokens_call(carried_d[0], carried[1], tok, w_first, wv.T)

    axes = ("dp", "ctx")
    scale = float(seq_rows * n * lax.axis_size("dp")) ** (-0.5)
    grad_second = sum(second)
    grad_down, grad_up, grad_gate, grad_second = lax.psum(
        (grad_down, grad_up, grad_gate, grad_second), axes
    )
    *cols, grad_value = lax.psum((*first_cols, grad_value), axes)
    return (
        carried[0].reshape(tokens.shape),
        grad_tokens.reshape(tokens.shape),
        jnp.concatenate([grad_gate, grad_value], axis=1) * scale,
        jnp.concatenate(cols, axis=1) * scale,
        grad_second * scale,
        grad_up * scale,
        grad_down * scale,
    )


def solution(mesh):
    placed = (P("dp", "ctx", None), P("dp", "ctx", None), P(), P(), P(), P(), P())
    return jax.shard_map(
        body,
        mesh=mesh,
        in_specs=placed,
        out_specs=(P("dp", "ctx", None), P("dp", "ctx", None), P(), P(), P(), P(), P()),
        check_vma=False,
    )
```

time: 923 us -> 706 us (0.76)
  matrix products: 294 us -> 0 us
  blocking collectives: 300 us -> 60.9 us
  waiting for transfers between devices: 156 us -> 348 us
  Pallas kernels: 0 us -> 191 us
  local copies, waits for them, and re-layouts: 118 us -> 18.7 us
  starting transfers between devices: 5 us -> 56.1 us
  other arithmetic: 28 us -> 14.3 us
    dot_general x15 -> x0, matrix products: 294 us -> none  [the longest x1 40.2 us: body(): jnp.einsum('mkc,im->ikc', d_mixed_mid, w_second, preferred_element_type=f32)]
    all_to_all x3 -> x2, blocking collectives: 300 us -> 60.9 us  [exchange(): lax.all_to_all(a.reshape(n, per // n, blocks, width), 'ctx', split_axis=0...]
    pallas_call x0 -> x19, Pallas kernels: none -> 191 us  [the longest x4 82.5 us: mlp_call(): pl.pallas_call(mlp_kernel, grid=(blocks // TILE,), in_specs=[tile, tile,...]
    all_to_all x1 -> x14, waiting for transfers between devices: 51.5 us -> 206 us  [exchange(): lax.all_to_all(a.reshape(n, per // n, blocks, width), 'ctx', split_axis=0...]
    all_to_all x1 -> x14, starting transfers between devices: 4.96 us -> 56 us  [exchange(): lax.all_to_all(a.reshape(n, per // n, blocks, width), 'ctx', split_axis=0...]
    convert_element_type x4 -> x0, local copies, waits for them, and re-layouts: 43.2 us -> none  [the longest x1 12.1 us: body(): d_first_mid = jnp.einsum('mkc,im->ikc', d_mixed_mid, w_second, preferred_...]
    psum x1, waiting for transfers between devices: 104 us -> 142 us  [body(): *cols, grad_value = lax.psum((*first_cols, grad_value), axes)]
    all_to_all x3 -> x0, local copies, waits for them, and re-layouts: 34 us -> none  [the longest x1 12.2 us: body(): lax.all_to_all(first, 'ctx', split_axis=1, concat_axis=0, tiled=True)]
  transfers between devices with their start and end apart: 2 -> 15, of which waited for: 2 -> 14; matrix products, arithmetic and copies ran while one was open for 8% -> 2% of each run, Pallas kernels for 0% -> 22%
where the time goes in v1:
time: 706 us; the launch traced here: 704 us
  waiting for transfers between devices  348 us (49%)
  Pallas kernels  191 us (27%)
  blocking collectives  60.9 us (9%)
  starting transfers between devices  56.1 us (8%)
  local copies, waits for them, and re-layouts  18.7 us (3%)
  other arithmetic  14.3 us (2%)
  between operations  14.3 us (2%)
    all_to_all x14, waiting for transfers between devices, exchange(): lax.all_to_all(a.reshape(n, per // n, blocks, width), 'ctx', split_axis=0...  206 us
    psum x1, waiting for transfers between devices, body(): *cols, grad_value = lax.psum((*first_cols, grad_value), axes)  142 us
    pallas_call x4, Pallas kernels, mlp_call(): pl.pallas_call(mlp_kernel, grid=(blocks // TILE,), in_specs=[tile, tile,...  82.5 us
    all_to_all x2, blocking collectives, exchange(): lax.all_to_all(a.reshape(n, per // n, blocks, width), 'ctx', split_axis=0...  60.9 us
    all_to_all x14, starting transfers between devices, exchange(): lax.all_to_all(a.reshape(n, per // n, blocks, width), 'ctx', split_axis=0...  56 us
    pallas_call x4, Pallas kernels, back_call(): pl.pallas_call(back_kernel, grid=(blocks // TILE,), in_specs=[pl.BlockSpe...  29.7 us
    pallas_call x4, Pallas kernels, mix_back_call(): pl.pallas_call(mix_back_kernel, grid=(per // count,), in_specs=[spec, spe...  25.1 us
    pallas_call x4, Pallas kernels, mix_call(): pl.pallas_call(mix_kernel, grid=(per // count,), in_specs=[spec, whole(w)...  19.2 us
  transfers between devices with their start and end apart: 15, of which 14 were waited for; matrix products, arithmetic and copies ran while one was open for 2% of the time, Pallas kernels for 22%

profile of v1, /device:TPU:0, one launch (start us, length us, event | category | flops | bytes accessed | tf_op | source)
XLA Modules:
  0.0 703.7 jit_solution(11412363918824882976)
XLA Ops:
  10.5 9.5 %values_first.1 = (bf16[64,512,128]{2,1,0:T(8,128)(2,1)}, bf16[128,64,128]{2,1,0:T(8,128)(2,1)}) custom-call(bf16[64,512,128]{2,1,0:T(8,128)(2,1)} %bitcast.26, bf16[128,128]{1,0:T(8,128)(2,1)} %get-tuple-element.111.refs_1_, bf16[128,512]{1,0:T(8,128)(2,1)} %slice.16.refs_2_), custom_call_target="tpu_custom_call" | custom-call | flops 2147483648 | bytes 18874368 | tf_op jit(solution)/shard_map/values_first/pallas_call | solution.py:73
  20.0 5.2 all-to-all-start.6
  26.0 9.0 %first_rest.1 = (bf16[128,64,128]{2,1,0:T(8,128)(2,1)}, bf16[128,64,128]{2,1,0:T(8,128)(2,1)}, bf16[128,64,128]{2,1,0:T(8,128)(2,1)}) custom-call(bf16[64,512,128]{2,1,0:T(8,128)(2,1)} %get-tuple-element.54.refs_0_.val, bf16[384,512]{1,0:T(8,128)(2,1)} %slice.17.refs_1_), custom_call_target="tpu_custom_call" | custom-call | flops 3221225472 | bytes 14680064 | tf_op jit(solution)/shard_map/first_rest/pallas_call | solution.py:83
  35.0 16.9 %all-to-all-done.6.x = bf16[8,16,64,128]{3,2,1,0:T(8,128)(2,1)S(1)} async-done(((bf16[8,16,64,128]{3,2,1,0:T(8,128)(2,1)}), bf16[8,16,64,128]{3,2,1,0:T(8,128)(2,1)S(1)}, u32[]{:S(2)}, u32[]{:S(2)}) %all-to-all-start.6) | async-done | bytes 2097184 | tf_op jit(solution)/shard_map/all_to_all | solution.py:304
  51.9 31.2 %all_to_all.80.x = bf16[8,16,64,128]{3,2,1,0:T(8,128)(2,1)} all-to-all(bf16[8,16,64,128]{3,2,1,0:T(8,128)(2,1)} %bitcast.55), channel_id=1, replica_groups=mesh['dp'=4,'ctx'=8] {'ctx'}, dimensions={0} | all-to-all | bytes 4194304 | tf_op jit(solution)/shard_map/all_to_all | solution.py:304
  83.1 29.7 %all_to_all.81.x = bf16[8,16,64,128]{3,2,1,0:T(8,128)(2,1)} all-to-all(bf16[8,16,64,128]{3,2,1,0:T(8,128)(2,1)S(1)} %bitcast.54), channel_id=1, replica_groups=mesh['dp'=4,'ctx'=8] {'ctx'}, dimensions={0} | all-to-all | bytes 4194304 | tf_op jit(solution)/shard_map/all_to_all | solution.py:304
  122.3 20.8 %all-to-all-done.4.x = bf16[8,16,64,128]{3,2,1,0:T(8,128)(2,1)S(1)} async-done(((bf16[8,16,64,128]{3,2,1,0:T(8,128)(2,1)}), bf16[8,16,64,128]{3,2,1,0:T(8,128)(2,1)S(1)}, u32[]{:S(2)}, u32[]{:S(2)}) %all-to-all-start.4) | async-done | bytes 2097184 | tf_op jit(solution)/shard_map/all_to_all | solution.py:304
  152.9 21.7 %all-to-all-done.7 = bf16[8,16,64,128]{3,2,1,0:T(8,128)(2,1)S(1)} async-done(((bf16[8,16,64,128]{3,2,1,0:T(8,128)(2,1)}), bf16[8,16,64,128]{3,2,1,0:T(8,128)(2,1)S(1)}, u32[]{:S(2)}, u32[]{:S(2)}) %all-to-all-start.7) | async-done | bytes 2097184 | tf_op jit(solution)/shard_map/all_to_all | solution.py:304
  184.3 21.8 %all-to-all-done.5 = bf16[8,16,64,128]{3,2,1,0:T(8,128)(2,1)S(1)} async-done(((bf16[8,16,64,128]{3,2,1,0:T(8,128)(2,1)}), bf16[8,16,64,128]{3,2,1,0:T(8,128)(2,1)S(1)}, u32[]{:S(2)}, u32[]{:S(2)}) %all-to-all-start.5) | async-done | bytes 2097184 | tf_op jit(solution)/shard_map/all_to_all | solution.py:304
  211.1 4.9 mix.5
  216.0 21.7 %all-to-all-done.1 = bf16[8,16,64,128]{3,2,1,0:T(8,128)(2,1)S(1)} async-done(((bf16[8,16,64,128]{3,2,1,0:T(8,128)(2,1)}), bf16[8,16,64,128]{3,2,1,0:T(8,128)(2,1)S(1)}, u32[]{:S(2)}, u32[]{:S(2)}) %all-to-all-start.1) | async-done | bytes 2097184 | tf_op jit(solution)/shard_map/all_to_all | solution.py:304
  245.5 20.6 %mlp.4 = (bf16[64,512,128]{2,1,0:T(8,128)(2,1)}, bf16[64,512,128]{2,1,0:T(8,128)(2,1)}, bf16[128,64,128]{2,1,0:T(8,128)(2,1)}, f32[256,128]{1,0:T(8,128)}, f32[128,256]{1,0:T(8,128)}, /*index=5*/f32[128,128]{1,0:T(8,128)}) custom-call(bf16[64,512,128]{2,1,0:T(8,128)(2,1)} %bitcast.27, bf16[64,512,128]{2,1,0:T(8,128)(2,1)} %bitcast.32, ...), custom_call_target="tpu_custom_call" | custom-call | flops 4026531840 | bytes 12582912 | tf_op jit(solution)/shard_map/mlp/pallas_call | solution.py:205
  273.6 20.6 %mlp.5 = (bf16[64,512,128]{2,1,0:T(8,128)(2,1)}, bf16[64,512,128]{2,1,0:T(8,128)(2,1)}, bf16[128,64,128]{2,1,0:T(8,128)(2,1)}, f32[256,128]{1,0:T(8,128)}, f32[128,256]{1,0:T(8,128)}, /*index=5*/f32[128,128]{1,0:T(8,128)}) custom-call(bf16[64,512,128]{2,1,0:T(8,128)(2,1)} %bitcast.28, ...), custom_call_target="tpu_custom_call", output_to_operand_aliasing={{0}: (9, {}), {1}: (10, {})} | custom-call | flops 4026531840 | bytes 12582912 | tf_op jit(solution)/shard_map/mlp/pallas_call | solution.py:205
  294.2 5.9 all-to-all-done.14.d
  305.9 20.6 %mlp.6 = (bf16[64,512,128]{2,1,0:T(8,128)(2,1)}, bf16[64,512,128]{2,1,0:T(8,128)(2,1)}, bf16[128,64,128]{2,1,0:T(8,128)(2,1)}, f32[256,128]{1,0:T(8,128)}, f32[128,256]{1,0:T(8,128)}, /*index=5*/f32[128,128]{1,0:T(8,128)}) custom-call(bf16[64,512,128]{2,1,0:T(8,128)(2,1)} %bitcast.29, ...), custom_call_target="tpu_custom_call", output_to_operand_aliasing={{0}: (9, {}), {1}: (10, {})} | custom-call | flops 4026531840 | bytes 12582912 | tf_op jit(solution)/shard_map/mlp/pallas_call | solution.py:205
  326.5 6.0 all-to-all-done.12.d
  336.3 20.7 %mlp.7 = (bf16[64,512,128]{2,1,0:T(8,128)(2,1)}, bf16[64,512,128]{2,1,0:T(8,128)(2,1)}, bf16[128,64,128]{2,1,0:T(8,128)(2,1)}, f32[256,128]{1,0:T(8,128)}, f32[128,256]{1,0:T(8,128)}, /*index=5*/f32[128,128]{1,0:T(8,128)}) custom-call(bf16[64,512,128]{2,1,0:T(8,128)(2,1)} %bitcast.30, ...), custom_call_target="tpu_custom_call", output_to_operand_aliasing={{0}: (9, {}), {1}: (10, {})} | custom-call | flops 4026531840 | bytes 12582912 | tf_op jit(solution)/shard_map/mlp/pallas_call | solution.py:205
  357.0 5.7 all-to-all-done.10.d
  368.4 6.3 mix_back.7
  374.7 20.3 %all-to-all-done.8.d = bf16[8,16,64,128]{3,2,1,0:T(8,128)(2,1)} async-done(((bf16[8,16,64,128]{3,2,1,0:T(8,128)(2,1)}), bf16[8,16,64,128]{3,2,1,0:T(8,128)(2,1)}, u32[]{:S(2)}, u32[]{:S(2)}) %all-to-all-start.8) | async-done | bytes 2097184 | tf_op jit(solution)/shard_map/all_to_all | solution.py:304
  398.7 6.3 mix_back.6
  404.9 20.3 %all-to-all-done.15 = bf16[8,16,64,128]{3,2,1,0:T(8,128)(2,1)S(1)} async-done(((bf16[8,16,64,128]{3,2,1,0:T(8,128)(2,1)}), bf16[8,16,64,128]{3,2,1,0:T(8,128)(2,1)S(1)}, u32[]{:S(2)}, u32[]{:S(2)}) %all-to-all-start.15) | async-done | bytes 2097184 | tf_op jit(solution)/shard_map/all_to_all | solution.py:304
  431.0 6.3 mix_back.5
  437.3 20.4 %all-to-all-done.13 = bf16[8,16,64,128]{3,2,1,0:T(8,128)(2,1)} async-done(((bf16[8,16,64,128]{3,2,1,0:T(8,128)(2,1)}), bf16[8,16,64,128]{3,2,1,0:T(8,128)(2,1)}, u32[]{:S(2)}, u32[]{:S(2)}) %all-to-all-start.13) | async-done | bytes 2097184 | tf_op jit(solution)/shard_map/all_to_all | solution.py:304
  461.2 6.3 mix_back.4
  467.5 20.3 %all-to-all-done.11 = bf16[8,16,64,128]{3,2,1,0:T(8,128)(2,1)S(1)} async-done(((bf16[8,16,64,128]{3,2,1,0:T(8,128)(2,1)}), bf16[8,16,64,128]{3,2,1,0:T(8,128)(2,1)S(1)}, u32[]{:S(2)}, u32[]{:S(2)}) %all-to-all-start.11) | async-done | bytes 2097184 | tf_op jit(solution)/shard_map/all_to_all | solution.py:304
  502.2 7.4 %first_back.4 = (bf16[64,512,128]{2,1,0:T(8,128)(2,1)}, f32[512,128]{1,0:T(8,128)}) custom-call(bf16[128,64,128]{2,1,0:T(8,128)(2,1)} %bitcast.42, bf16[64,512,128]{2,1,0:T(8,128)(2,1)} %get-tuple-element.54.refs_0_.val), custom_call_target="tpu_custom_call" | custom-call | flops 1073741824 | bytes 12582912 | tf_op jit(solution)/shard_map/first_back/pallas_call | solution.py:235
  509.6 7.4 %first_back.5 = (bf16[64,512,128]{2,1,0:T(8,128)(2,1)}, f32[512,128]{1,0:T(8,128)}) custom-call(bf16[128,64,128]{2,1,0:T(8,128)(2,1)} %bitcast.21.d, bf16[64,512,128]{2,1,0:T(8,128)(2,1)} %get-tuple-element.54.refs_0_.val, bf16[64,512,128]{2,1,0:T(8,128)(2,1)} %get-tuple-element.74.rest_0_), custom_call_target="tpu_custom_call", output_to_operand_aliasing={{0}: (2, {})} | custom-call | flops 1073741824 | bytes 12582912 | tf_op jit(solution)/shard_map/first_back/pallas_call | solution.py:235
  517.1 7.4 %first_back.6 = (bf16[64,512,128]{2,1,0:T(8,128)(2,1)}, f32[512,128]{1,0:T(8,128)}) custom-call(bf16[128,64,128]{2,1,0:T(8,128)(2,1)} %bitcast.43, bf16[64,512,128]{2,1,0:T(8,128)(2,1)} %get-tuple-element.54.refs_0_.val, bf16[64,512,128]{2,1,0:T(8,128)(2,1)} %get-tuple-element.75.rest_0_), custom_call_target="tpu_custom_call", output_to_operand_aliasing={{0}: (2, {})} | custom-call | flops 1073741824 | bytes 12582912 | tf_op jit(solution)/shard_map/first_back/pallas_call | solution.py:235
  524.5 7.5 %first_back.7 = (bf16[64,512,128]{2,1,0:T(8,128)(2,1)}, f32[512,128]{1,0:T(8,128)}) custom-call(bf16[128,64,128]{2,1,0:T(8,128)(2,1)} %bitcast.17.d, bf16[64,512,128]{2,1,0:T(8,128)(2,1)} %get-tuple-element.54.refs_0_.val, bf16[64,512,128]{2,1,0:T(8,128)(2,1)} %get-tuple-element.76.rest_0_), custom_call_target="tpu_custom_call", output_to_operand_aliasing={{0}: (2, {})} | custom-call | flops 1073741824 | bytes 12582912 | tf_op jit(solution)/shard_map/first_back/pallas_call | solution.py:235
  532.0 16.2 %grad_tokens.1 = (bf16[64,512,128]{2,1,0:T(8,128)(2,1)}, f32[128,128]{1,0:T(8,128)}) custom-call(bf16[64,512,128]{2,1,0:T(8,128)(2,1)} %get-tuple-element.77.d, bf16[64,512,128]{2,1,0:T(8,128)(2,1)} %get-tuple-element.78.part, bf16[64,512,128]{2,1,0:T(8,128)(2,1)} %bitcast.31, bf16[512,512]{1,0:T(8,128)(2,1)} %w1.1, bf16[128,128]{1,0:T(8,128)(2,1)} %bitcast.68), custom_call_target="tpu_custom_call" | custom-call | flops 6442450944 | bytes 33554432 | tf_op jit(solution)/shard_map/grad_tokens/pallas_call | solution.py:277
  548.2 142.3 %all-reduce.3.cloned.1.call-done = (f32[128,128]{1,0:T(8,128)}, f32[128,128]{1,0:T(8,128)}, f32[512,128]{1,0:T(8,128)}, f32[512,128]{1,0:T(8,128)}, f32[512,128]...) async-done(((f32[128,128]{1,0:T(8,128)}, f32[128,128]{1,0:T(8,128)}, f32[512,128]{1,0:T(8,128)}, ...) | async-done | bytes 2490384 | tf_op jit(solution)/shard_map/psum | solution.py:345
  (76 shorter events, 102.1 us)
Async XLA Ops:
  8.6 236.3 %copy-start.12 = (bf16[128,128]{1,0:T(8,128)(2,1)}, bf16[128,128]{1,0:T(8,128)(2,1)S(1)}, u32[]{:S(2)}) copy-start(bf16[128,128]{1,0:T(8,128)(2,1)S(1)} %get-tuple-element.110.wg) | copy-start | bytes 98308
  20.0 31.8 %all-to-all-start.6 = ((bf16[8,16,64,128]{3,2,1,0:T(8,128)(2,1)}), bf16[8,16,64,128]{3,2,1,0:T(8,128)(2,1)S(1)}, u32[]{:S(2)}, u32[]{:S(2)}) async-start(bf16[8,16,64,128]{3,2,1,0:T(8,128)(2,1)} %bitcast.53), calls=%async_computation.6 | async-start | bytes 4194304 | tf_op jit(solution)/shard_map/all_to_all | solution.py:304
  51.9 31.2 %copy-start.5 = (bf16[8,16,64,128]{3,2,1,0:T(8,128)(2,1)}, bf16[8,16,64,128]{3,2,1,0:T(8,128)(2,1)S(1)}, u32[]{:S(2)}) copy-start(bf16[8,16,64,128]{3,2,1,0:T(8,128)(2,1)S(1)} %all-to-all-done.6.x) | copy-start | bytes 6291460
  51.9 31.2 %copy-start.9 = (bf16[128,64,128]{2,1,0:T(8,128)(2,1)S(1)}, bf16[128,64,128]{2,1,0:T(8,128)(2,1)}, u32[]{:S(2)}) copy-start(bf16[128,64,128]{2,1,0:T(8,128)(2,1)} %get-tuple-element.55) | copy-start | bytes 6291460
  112.8 3.7 copy-start.15
  112.8 30.3 %all-to-all-start.4 = ((bf16[8,16,64,128]{3,2,1,0:T(8,128)(2,1)}), bf16[8,16,64,128]{3,2,1,0:T(8,128)(2,1)S(1)}, u32[]{:S(2)}, u32[]{:S(2)}) async-start(bf16[8,16,64,128]{3,2,1,0:T(8,128)(2,1)} %bitcast.52), calls=%async_computation.4 | async-start | bytes 4194304 | tf_op jit(solution)/shard_map/all_to_all | solution.py:304
  144.4 30.2 %all-to-all-start.7 = ((bf16[8,16,64,128]{3,2,1,0:T(8,128)(2,1)}), bf16[8,16,64,128]{3,2,1,0:T(8,128)(2,1)S(1)}, u32[]{:S(2)}, u32[]{:S(2)}) async-start(bf16[8,16,64,128]{3,2,1,0:T(8,128)(2,1)} %mix.7), calls=%async_computation.7 | async-start | bytes 4194304 | tf_op jit(solution)/shard_map/all_to_all | solution.py:304
  174.6 1.3 copy-start.4
  175.9 30.2 %all-to-all-start.5 = ((bf16[8,16,64,128]{3,2,1,0:T(8,128)(2,1)}), bf16[8,16,64,128]{3,2,1,0:T(8,128)(2,1)S(1)}, u32[]{:S(2)}, u32[]{:S(2)}) async-start(bf16[8,16,64,128]{3,2,1,0:T(8,128)(2,1)} %mix.6), calls=%async_computation.5 | async-start | bytes 4194304 | tf_op jit(solution)/shard_map/all_to_all | solution.py:304
  207.4 30.2 %all-to-all-start.1 = ((bf16[8,16,64,128]{3,2,1,0:T(8,128)(2,1)}), bf16[8,16,64,128]{3,2,1,0:T(8,128)(2,1)S(1)}, u32[]{:S(2)}, u32[]{:S(2)}) async-start(bf16[8,16,64,128]{3,2,1,0:T(8,128)(2,1)} %mix.4), calls=%async_computation.1 | async-start | bytes 4194304 | tf_op jit(solution)/shard_map/all_to_all | solution.py:304
  216.0 27.4 %copy-start.10 = (bf16[128,256]{1,0:T(8,128)(2,1)S(1)}, bf16[128,256]{1,0:T(8,128)(2,1)}, u32[]{:S(2)}) copy-start(bf16[128,256]{1,0:T(8,128)(2,1)} %wu.7) | copy-start | bytes 196612
  216.0 28.1 %copy-start.11 = (bf16[256,128]{1,0:T(8,128)(2,1)S(1)}, bf16[256,128]{1,0:T(8,128)(2,1)}, u32[]{:S(2)}) copy-start(bf16[256,128]{1,0:T(8,128)(2,1)} %wd.7) | copy-start | bytes 196612
  237.6 1.3 copy-start
  239.0 31.0 %all-to-all-start.3 = ((bf16[8,16,64,128]{3,2,1,0:T(8,128)(2,1)}), bf16[8,16,64,128]{3,2,1,0:T(8,128)(2,1)}, u32[]{:S(2)}, u32[]{:S(2)}) async-start(bf16[8,16,64,128]{3,2,1,0:T(8,128)(2,1)} %mix.5), calls=%async_computation.3 | async-start | bytes 4194304 | tf_op jit(solution)/shard_map/all_to_all | solution.py:304
  270.0 30.2 %all-to-all-start.14 = ((bf16[8,16,64,128]{3,2,1,0:T(8,128)(2,1)}), bf16[8,16,64,128]{3,2,1,0:T(8,128)(2,1)S(1)}, u32[]{:S(2)}, u32[]{:S(2)}) async-start(bf16[8,16,64,128]{3,2,1,0:T(8,128)(2,1)} %bitcast.51), calls=%async_computation.14 | async-start | bytes 4194304 | tf_op jit(solution)/shard_map/all_to_all | solution.py:304
  300.2 1.4 copy-start.7
  301.5 31.0 %all-to-all-start.12 = ((bf16[8,16,64,128]{3,2,1,0:T(8,128)(2,1)}), bf16[8,16,64,128]{3,2,1,0:T(8,128)(2,1)}, u32[]{:S(2)}, u32[]{:S(2)}) async-start(bf16[8,16,64,128]{3,2,1,0:T(8,128)(2,1)} %bitcast.50), calls=%async_computation.12 | async-start | bytes 4194304 | tf_op jit(solution)/shard_map/all_to_all | solution.py:304
  332.5 30.2 %all-to-all-start.10 = ((bf16[8,16,64,128]{3,2,1,0:T(8,128)(2,1)}), bf16[8,16,64,128]{3,2,1,0:T(8,128)(2,1)S(1)}, u32[]{:S(2)}, u32[]{:S(2)}) async-start(bf16[8,16,64,128]{3,2,1,0:T(8,128)(2,1)} %bitcast.48), calls=%async_computation.10 | async-start | bytes 4194304 | tf_op jit(solution)/shard_map/all_to_all | solution.py:304
  362.7 1.3 copy-start.8
  364.1 31.0 %all-to-all-start.8 = ((bf16[8,16,64,128]{3,2,1,0:T(8,128)(2,1)}), bf16[8,16,64,128]{3,2,1,0:T(8,128)(2,1)}, u32[]{:S(2)}, u32[]{:S(2)}) async-start(bf16[8,16,64,128]{3,2,1,0:T(8,128)(2,1)} %bitcast.49), calls=%async_computation.8 | async-start | bytes 4194304 | tf_op jit(solution)/shard_map/all_to_all | solution.py:304
  395.1 30.2 %all-to-all-start.15 = ((bf16[8,16,64,128]{3,2,1,0:T(8,128)(2,1)}), bf16[8,16,64,128]{3,2,1,0:T(8,128)(2,1)S(1)}, u32[]{:S(2)}, u32[]{:S(2)}) async-start(bf16[8,16,64,128]{3,2,1,0:T(8,128)(2,1)} %get-tuple-element.73), calls=%async_computation.15 | async-start | bytes 4194304 | tf_op jit(solution)/shard_map/all_to_all | solution.py:304
  425.2 1.4 copy-start.1
  426.6 31.0 %all-to-all-start.13 = ((bf16[8,16,64,128]{3,2,1,0:T(8,128)(2,1)}), bf16[8,16,64,128]{3,2,1,0:T(8,128)(2,1)}, u32[]{:S(2)}, u32[]{:S(2)}) async-start(bf16[8,16,64,128]{3,2,1,0:T(8,128)(2,1)} %get-tuple-element.71), calls=%async_computation.13 | async-start | bytes 4194304 | tf_op jit(solution)/shard_map/all_to_all | solution.py:304
  457.6 30.2 %all-to-all-start.11 = ((bf16[8,16,64,128]{3,2,1,0:T(8,128)(2,1)}), bf16[8,16,64,128]{3,2,1,0:T(8,128)(2,1)S(1)}, u32[]{:S(2)}, u32[]{:S(2)}) async-start(bf16[8,16,64,128]{3,2,1,0:T(8,128)(2,1)} %get-tuple-element.69), calls=%async_computation.11 | async-start | bytes 4194304 | tf_op jit(solution)/shard_map/all_to_all | solution.py:304
  487.8 5.7 copy-start.16
  487.8 6.4 copy-start.19
  487.8 8.0 %copy-start.18 = (f32[256,128]{1,0:T(8,128)S(1)}, f32[256,128]{1,0:T(8,128)}, u32[]{:S(2)}) copy-start(f32[256,128]{1,0:T(8,128)} %get-tuple-element.97) | copy-start | bytes 393220
  487.8 9.7 %copy-start.17 = (f32[128,256]{1,0:T(8,128)S(1)}, f32[128,256]{1,0:T(8,128)}, u32[]{:S(2)}) copy-start(f32[128,256]{1,0:T(8,128)} %get-tuple-element.93) | copy-start | bytes 393220
  487.8 11.4 %copy-start.13 = (f32[512,512]{1,0:T(8,128)S(1)}, f32[512,512]{1,0:T(8,128)}, u32[]{:S(2)}) copy-start(f32[512,512]{1,0:T(8,128)} %get-tuple-element.89) | copy-start | bytes 3145732
  489.1 35.4 %all-to-all-start.9 = ((bf16[8,16,64,128]{3,2,1,0:T(8,128)(2,1)}), bf16[8,16,64,128]{3,2,1,0:T(8,128)(2,1)}, u32[]{:S(2)}, u32[]{:S(2)}) async-start(bf16[8,16,64,128]{3,2,1,0:T(8,128)(2,1)} %get-tuple-element.67), calls=%async_computation.9 | async-start | bytes 4194304 | tf_op jit(solution)/shard_map/all_to_all | solution.py:304
  493.5 5.8 copy-start.14
  493.5 197.0 %all-reduce.3.cloned.1.call-start = ((), (), s32[]{:S(2)}) async-start(), calls=%async_computation.16 | async-start | bytes 4980736 | tf_op jit(solution)/shard_map/psum | solution.py:345
  (3 other events, 3.9 us)
Sparse Core Ops, SparseCore 0:
  548.3 142.1 all-reduce.2

commit v2 on v1

--- a/solution.py
+++ b/solution.py
@@ -155,7 +155,7 @@
     out, part, dmix, gdown, gup, ggate, mixed, dback = rest[-8:]
     width = tok.shape[2]
     steps = tok.shape[1]
-    sub = 4
+    sub = 2
 
     @pl.when(pl.program_id(0) == 0)
     def _():
@@ -217,8 +217,7 @@
     )(tokens, cot, mix, *weights, *carried)
 
 
-def back_kernel(d, val, *rest):
-    out, grad = rest[-2:]
+def back_kernel(d, val, out, grad):
 
     @pl.when(pl.program_id(0) == 0)
     def _():
@@ -228,41 +227,39 @@
     grad[...] += dot_lanes(lanes(val, TILE), lanes(out, TILE))
 
 
-def back_call(chunk, d, values, carried):
+def back_call(d, values):
     blocks, steps, width = values.shape
     per = d.shape[0]
-    held = [pl.BlockSpec(memory_space=pl.ANY)] * len(carried)
     return pl.pallas_call(
         back_kernel,
         grid=(blocks // TILE,),
         in_specs=[
             pl.BlockSpec((per, TILE, width), lambda t: (0, t, 0)),
             pl.BlockSpec((TILE, steps, width), lambda t: (t, 0, 0)),
-        ]
-        + held,
+        ],
         out_specs=[
-            pl.BlockSpec((TILE, per, width), lambda t: (t, chunk, 0)),
+            pl.BlockSpec((TILE, per, width), lambda t: (t, 0, 0)),
             pl.BlockSpec((steps, per), lambda t: (0, 0)),
         ],
         out_shape=[
-            jax.ShapeDtypeStruct(values.shape, BF16),
+            jax.ShapeDtypeStruct((blocks, per, width), BF16),
             jax.ShapeDtypeStruct((steps, per), F32),
         ],
-        input_output_aliases={2 + a: a for a in range(len(carried))},
         compiler_params=params(),
         cost_estimate=cost(2 * values.size * per, 2 * values.size + 4 * d.size),
         name="first_back",
-    )(d, values, *carried)
-
-
-def tokens_kernel(d, part, tok, w1, wvt, out, grad):
+    )(d, values)
+
+
+def tokens_kernel(*refs):
+    *ds, part, tok, w1, wvt, out, grad = refs
     width = tok.shape[2]
 
     @pl.when(pl.program_id(0) == 0)
     def _():
         grad[...] = jnp.zeros_like(grad)
 
-    res = dot(w1[...], lanes(d, TILE))
+    res = dot(w1[...], jnp.concatenate([lanes(d, TILE) for d in ds], axis=0))
     total = grad[...]
     for b in range(TILE):
         dv = res[:, b * width : (b + 1) * width].astype(BF16)
@@ -271,19 +268,42 @@
     grad[...] = total
 
 
-def tokens_call(d, part, tokens, w1, wvt):
+def tokens_call(ds, part, tokens, w1, wvt):
     blocks, steps, width = tokens.shape
     tile = pl.BlockSpec((TILE, steps, width), lambda t: (t, 0, 0))
     return pl.pallas_call(
         tokens_kernel,
         grid=(blocks // TILE,),
-        in_specs=[tile, tile, tile, whole(w1), whole(wvt)],
+        in_specs=[pl.BlockSpec((TILE, *d.shape[1:]), lambda t: (t, 0, 0)) for d in ds]
+        + [tile, tile, whole(w1), whole(wvt)],
         out_specs=[tile, whole(wvt)],
         out_shape=[jax.ShapeDtypeStruct(tokens.shape, BF16), jax.ShapeDtypeStruct(wvt.shape, F32)],
         compiler_params=params(),
         cost_estimate=cost(2 * tokens.size * (steps + 2 * width), 8 * tokens.size),
         name="grad_tokens",
-    )(d, part, tokens, w1, wvt)
+    )(*ds, part, tokens, w1, wvt)
+
+
+def summed_late(parts):
+    rows = sum(p.shape[0] for p in parts)
+    width = parts[0].shape[1]
+    n = lax.axis_size("ctx")
+
+    def swap(a, axis):
+        return lax.all_to_all(a, axis, split_axis=0, concat_axis=0, tiled=True)
+
+    def spread(a, axis):
+        return swap(jnp.broadcast_to(a, (lax.axis_size(axis), *a.shape)), axis)
+
+    mine = swap(jnp.concatenate(parts, axis=0).astype(BF16).reshape(n, rows // n, width), "ctx")
+    mine = jnp.sum(mine.astype(F32), axis=0).astype(BF16)
+    mine = jnp.sum(spread(mine, "dp").astype(F32), axis=0).astype(BF16)
+    total = spread(mine, "ctx").reshape(rows, width).astype(F32)
+    out, at = [], 0
+    for p in parts:
+        out.append(total[at : at + p.shape[0]])
+        at += p.shape[0]
+    return out
 
 
 def body(tokens, cotangent, w_gate_value, w_first, w_second, w_up, w_down):
@@ -291,7 +311,7 @@
     seq_rows, width = tokens.shape[1:]
     steps = w_first.shape[0]
     blocks = seq_rows // steps
-    chunks = 4
+    chunks = 2
     per = steps // chunks
     tok = tokens.reshape(blocks, steps, width)
     cot = cotangent.reshape(blocks, steps, width)
@@ -311,7 +331,7 @@
 
     first_mid, mixed, d_mixed, d_first = {}, {}, {}, {}
     small, second, first_cols = [], [], []
-    carried, carried_d = (), ()
+    carried = ()
     for at in range(chunks + 3):
         if at < chunks:
             first_mid[at] = exchange(firsts[at])
@@ -329,12 +349,13 @@
             df, g2 = mix_back_call(first_mid[c], d_mixed[c], w_second)
             second.append(g2)
             d_first[c] = exchange(df).reshape(per, blocks, width)
+    back = []
     for c in range(chunks):
-        filled, cols = back_call(c, d_first[c], values, carried_d)
-        carried_d = (filled,)
+        filled, cols = back_call(d_first[c], values)
+        back.append(filled)
         first_cols.append(cols)
     grad_down, grad_up, grad_gate = [sum(parts) for parts in zip(*small)]
-    grad_tokens, grad_value = tokens_call(carried_d[0], carried[1], tok, w_first, wv.T)
+    grad_tokens, grad_value = tokens_call(back, carried[1], tok, w_first, wv.T)
 
     axes = ("dp", "ctx")
     scale = float(seq_rows * n * lax.axis_size("dp")) ** (-0.5)
@@ -342,12 +363,13 @@
     grad_down, grad_up, grad_gate, grad_second = lax.psum(
         (grad_down, grad_up, grad_gate, grad_second), axes
     )
-    *cols, grad_value = lax.psum((*first_cols, grad_value), axes)
+    strips = [c[:, at : at + width] for c in first_cols for at in range(0, per, width)]
+    *strips, grad_value = summed_late([*strips, grad_value])
     return (
         carried[0].reshape(tokens.shape),
         grad_tokens.reshape(tokens.shape),
         jnp.concatenate([grad_gate, grad_value], axis=1) * scale,
-        jnp.concatenate(cols, axis=1) * scale,
+        jnp.concatenate(strips, axis=1) * scale,
         grad_second * scale,
         grad_up * scale,
         grad_down * scale,

time: 706 us -> 619 us (0.88)
  waiting for transfers between devices: 348 us -> 304 us
  Pallas kernels: 191 us -> 168 us
  starting transfers between devices: 56.1 us -> 42.5 us
  local copies, waits for them, and re-layouts: 18.7 us -> 9.23 us
    psum x1, waiting for transfers between devices: 142 us -> 52 us  [body(): lax.psum((grad_down, grad_up, grad_gate, grad_second), axes)]
    all_to_all x14 -> x7, waiting for transfers between devices: 206 us -> 246 us  [exchange(): lax.all_to_all(a.reshape(n, per // n, blocks, width), 'ctx', split_axis=0...]
    all_to_all x14 -> x7, starting transfers between devices: 56 us -> 33 us  [exchange(): lax.all_to_all(a.reshape(n, per // n, blocks, width), 'ctx', split_axis=0...]
    pallas_call x4 -> x2, Pallas kernels: 29.7 us -> 17 us  [back_call(): pl.pallas_call(back_kernel, grid=(blocks // TILE,), in_specs=[pl.BlockSpe...]
    all_to_all x0 -> x1, blocking collectives: none -> 12.6 us  [swap(): return lax.all_to_all(a, axis, split_axis=0, concat_axis=0, tiled=True)]
    unnamed x46 -> x40, local copies, waits for them, and re-layouts: 15.9 us -> 5.31 us
    all_to_all x0 -> x2, starting transfers between devices: none -> 9.21 us  [swap(): return lax.all_to_all(a, axis, split_axis=0, concat_axis=0, tiled=True)]
    all_to_all x2 -> x1, blocking collectives: 60.9 us -> 53.6 us  [exchange(): lax.all_to_all(a.reshape(n, per // n, blocks, width), 'ctx', split_axis=0...]
  transfers between devices with their start and end apart: 15 -> 10, of which waited for: 14 -> 9; matrix products, arithmetic and copies ran while one was open for 2% -> 2% of each run, Pallas kernels for 22% -> 19%
where the time goes in v2:
time: 619 us; the launch traced here: 617 us
  waiting for transfers between devices  304 us (49%)
  Pallas kernels  168 us (27%)
  blocking collectives  66.1 us (11%)
  starting transfers between devices  42.5 us (7%)
  between operations  14.3 us (2%)
  other arithmetic  12.5 us (2%)
  local copies, waits for them, and re-layouts  9.23 us (1%)
    all_to_all x7, waiting for transfers between devices, exchange(): lax.all_to_all(a.reshape(n, per // n, blocks, width), 'ctx', split_axis=0...  246 us
    pallas_call x2, Pallas kernels, mlp_call(): pl.pallas_call(mlp_kernel, grid=(blocks // TILE,), in_specs=[tile, tile,...  79.1 us
    all_to_all x1, blocking collectives, exchange(): lax.all_to_all(a.reshape(n, per // n, blocks, width), 'ctx', split_axis=0...  53.6 us
    psum x1, waiting for transfers between devices, body(): lax.psum((grad_down, grad_up, grad_gate, grad_second), axes)  52 us
    all_to_all x7, starting transfers between devices, exchange(): lax.all_to_all(a.reshape(n, per // n, blocks, width), 'ctx', split_axis=0...  33 us
    pallas_call x2, Pallas kernels, mix_back_call(): pl.pallas_call(mix_back_kernel, grid=(per // count,), in_specs=[spec, spe...  21.3 us
    pallas_call x2, Pallas kernels, back_call(): pl.pallas_call(back_kernel, grid=(blocks // TILE,), in_specs=[pl.BlockSpe...  17 us
    pallas_call x2, Pallas kernels, mix_call(): pl.pallas_call(mix_kernel, grid=(per // count,), in_specs=[spec, whole(w)...  16.4 us
  transfers between devices with their start and end apart: 10, of which 9 were waited for; matrix products, arithmetic and copies ran while one was open for 2% of the time, Pallas kernels for 19%

profile of v2, /device:TPU:0, one launch (start us, length us, event | category | flops | bytes accessed | tf_op | source)
XLA Modules:
  0.0 617.2 jit_solution(8103701162828072089)
XLA Ops:
  10.7 10.8 %values_first.1 = (bf16[64,512,128]{2,1,0:T(8,128)(2,1)}, bf16[256,64,128]{2,1,0:T(8,128)(2,1)}) custom-call(bf16[64,512,128]{2,1,0:T(8,128)(2,1)} %bitcast.22, bf16[128,128]{1,0:T(8,128)(2,1)} %get-tuple-element.66.refs_1_, bf16[256,512]{1,0:T(8,128)(2,1)} %get-tuple-element.64.refs_2_), custom_call_target="tpu_custom_call" | custom-call | flops 3221225472 | bytes 20971520 | tf_op jit(solution)/shard_map/values_first/pallas_call | solution.py:73
  21.5 5.2 all-to-all-start.2
  26.6 7.5 %first_rest.1 = bf16[256,64,128]{2,1,0:T(8,128)(2,1)} custom-call(bf16[64,512,128]{2,1,0:T(8,128)(2,1)} %get-tuple-element.31.refs_0_.val, bf16[256,512]{1,0:T(8,128)(2,1)} %get-tuple-element.63.refs_1_), custom_call_target="tpu_custom_call" | custom-call | flops 2147483648 | bytes 12582912 | tf_op jit(solution)/shard_map/first_rest/pallas_call | solution.py:83
  34.2 41.7 %all-to-all-done.2.x = bf16[8,32,64,128]{3,2,1,0:T(8,128)(2,1)} async-done(((bf16[8,32,64,128]{3,2,1,0:T(8,128)(2,1)}), bf16[8,32,64,128]{3,2,1,0:T(8,128)(2,1)}, u32[]{:S(2)}, u32[]{:S(2)}) %all-to-all-start.2) | async-done | bytes 4194336 | tf_op jit(solution)/shard_map/all_to_all | solution.py:324
  75.9 4.7 all-to-all-start
  81.6 8.2 %mix.3 = bf16[8,32,64,128]{3,2,1,0:T(8,128)(2,1)} custom-call(bf16[8,32,64,128]{3,2,1,0:T(8,128)(2,1)} %all-to-all-done.2.x, bf16[512,512]{1,0:T(8,128)(2,1)} %bitcast.30), custom_call_target="tpu_custom_call" | custom-call | flops 2147483648 | bytes 8388608 | tf_op jit(solution)/shard_map/mix/pallas_call | solution.py:126
  89.8 39.9 %all-to-all-done.x = bf16[8,32,64,128]{3,2,1,0:T(8,128)(2,1)} async-done(((bf16[8,32,64,128]{3,2,1,0:T(8,128)(2,1)}), bf16[8,32,64,128]{3,2,1,0:T(8,128)(2,1)}, u32[]{:S(2)}, u32[]{:S(2)}) %all-to-all-start) | async-done | bytes 4194336 | tf_op jit(solution)/shard_map/all_to_all | solution.py:324
  129.7 4.6 all-to-all-start.3
  134.3 8.3 %mix.2 = bf16[8,32,64,128]{3,2,1,0:T(8,128)(2,1)} custom-call(bf16[8,32,64,128]{3,2,1,0:T(8,128)(2,1)} %all-to-all-done.x, bf16[512,512]{1,0:T(8,128)(2,1)} %bitcast.31), custom_call_target="tpu_custom_call" | custom-call | flops 2147483648 | bytes 8388608 | tf_op jit(solution)/shard_map/mix/pallas_call | solution.py:126
  142.6 40.9 %all-to-all-done.3 = bf16[8,32,64,128]{3,2,1,0:T(8,128)(2,1)} async-done(((bf16[8,32,64,128]{3,2,1,0:T(8,128)(2,1)}), bf16[8,32,64,128]{3,2,1,0:T(8,128)(2,1)}, u32[]{:S(2)}, u32[]{:S(2)}) %all-to-all-start.3) | async-done | bytes 4194336 | tf_op jit(solution)/shard_map/all_to_all | solution.py:324
  183.4 4.6 all-to-all-start.1
  190.2 39.5 %mlp.2 = (bf16[64,512,128]{2,1,0:T(8,128)(2,1)}, bf16[64,512,128]{2,1,0:T(8,128)(2,1)}, bf16[256,64,128]{2,1,0:T(8,128)(2,1)}, f32[256,128]{1,0:T(8,128)}, f32[128,256]{1,0:T(8,128)}, /*index=5*/f32[128,128]{1,0:T(8,128)}) custom-call(bf16[64,512,128]{2,1,0:T(8,128)(2,1)} %bitcast.23, bf16[64,512,128]{2,1,0:T(8,128)(2,1)} %bitcast.27, ...), custom_call_target="tpu_custom_call" | custom-call | flops 8053063680 | bytes 25165824 | tf_op jit(solution)/shard_map/mlp/pallas_call | solution.py:205
  229.7 7.4 %all-to-all-done.1 = bf16[8,32,64,128]{3,2,1,0:T(8,128)(2,1)} async-done(((bf16[8,32,64,128]{3,2,1,0:T(8,128)(2,1)}), bf16[8,32,64,128]{3,2,1,0:T(8,128)(2,1)}, u32[]{:S(2)}, u32[]{:S(2)}) %all-to-all-start.1) | async-done | bytes 4194336 | tf_op jit(solution)/shard_map/all_to_all | solution.py:324
  237.1 39.5 %mlp.3 = (bf16[64,512,128]{2,1,0:T(8,128)(2,1)}, bf16[64,512,128]{2,1,0:T(8,128)(2,1)}, bf16[256,64,128]{2,1,0:T(8,128)(2,1)}, f32[256,128]{1,0:T(8,128)}, f32[128,256]{1,0:T(8,128)}, /*index=5*/f32[128,128]{1,0:T(8,128)}) custom-call(bf16[64,512,128]{2,1,0:T(8,128)(2,1)} %bitcast.24, ...), custom_call_target="tpu_custom_call", output_to_operand_aliasing={{0}: (9, {}), {1}: (10, {})} | custom-call | flops 8053063680 | bytes 25165824 | tf_op jit(solution)/shard_map/mlp/pallas_call | solution.py:205
  276.7 53.6 %all_to_all.55.d = bf16[8,32,64,128]{3,2,1,0:T(8,128)(2,1)} all-to-all(bf16[8,32,64,128]{3,2,1,0:T(8,128)(2,1)} %bitcast.33), channel_id=1, replica_groups=mesh['dp'=4,'ctx'=8] {'ctx'}, dimensions={0} | all-to-all | bytes 8388608 | tf_op jit(solution)/shard_map/all_to_all | solution.py:324
  330.2 4.6 all-to-all-start.4
  334.8 10.7 %mix_back.3 = (bf16[8,32,64,128]{3,2,1,0:T(8,128)(2,1)}, f32[512,512]{1,0:T(8,128)}) custom-call(bf16[8,32,64,128]{3,2,1,0:T(8,128)(2,1)} %all-to-all-done.x, bf16[8,32,64,128]{3,2,1,0:T(8,128)(2,1)} %all_to_all.55.d, bf16[512,512]{1,0:T(8,128)(2,1)} %w.3), custom_call_target="tpu_custom_call" | custom-call | flops 4294967296 | bytes 12582912 | tf_op jit(solution)/shard_map/mix_back/pallas_call | solution.py:142
  345.5 38.4 %all-to-all-done.4.d = bf16[8,32,64,128]{3,2,1,0:T(8,128)(2,1)} async-done(((bf16[8,32,64,128]{3,2,1,0:T(8,128)(2,1)}), bf16[8,32,64,128]{3,2,1,0:T(8,128)(2,1)}, u32[]{:S(2)}, u32[]{:S(2)}) %all-to-all-start.4) | async-done | bytes 4194336 | tf_op jit(solution)/shard_map/all_to_all | solution.py:324
  383.9 4.6 all-to-all-start.7
  388.5 10.7 %mix_back.2 = (bf16[8,32,64,128]{3,2,1,0:T(8,128)(2,1)}, f32[512,512]{1,0:T(8,128)}) custom-call(bf16[8,32,64,128]{3,2,1,0:T(8,128)(2,1)} %all-to-all-done.2.x, bf16[8,32,64,128]{3,2,1,0:T(8,128)(2,1)} %all-to-all-done.4.d, bf16[512,512]{1,0:T(8,128)(2,1)} %w.3), custom_call_target="tpu_custom_call" | custom-call | flops 4294967296 | bytes 12582912 | tf_op jit(solution)/shard_map/mix_back/pallas_call | solution.py:142
  399.2 38.4 %all-to-all-done.7 = bf16[8,32,64,128]{3,2,1,0:T(8,128)(2,1)} async-done(((bf16[8,32,64,128]{3,2,1,0:T(8,128)(2,1)}), bf16[8,32,64,128]{3,2,1,0:T(8,128)(2,1)}, u32[]{:S(2)}, u32[]{:S(2)}) %all-to-all-start.7) | async-done | bytes 4194336 | tf_op jit(solution)/shard_map/all_to_all | solution.py:324
  437.7 4.9 all-to-all-start.5
  446.7 8.5 %first_back.3 = (bf16[64,256,128]{2,1,0:T(8,128)(2,1)}, f32[512,256]{1,0:T(8,128)}) custom-call(bf16[256,64,128]{2,1,0:T(8,128)(2,1)} %bitcast.15.d, bf16[64,512,128]{2,1,0:T(8,128)(2,1)} %get-tuple-element.31.refs_0_.val), custom_call_target="tpu_custom_call" | custom-call | flops 2147483648 | bytes 16777216 | tf_op jit(solution)/shard_map/first_back/pallas_call | solution.py:233
  455.2 39.5 %all-to-all-done.5 = bf16[8,32,64,128]{3,2,1,0:T(8,128)(2,1)} async-done(((bf16[8,32,64,128]{3,2,1,0:T(8,128)(2,1)}), bf16[8,32,64,128]{3,2,1,0:T(8,128)(2,1)}, u32[]{:S(2)}, u32[]{:S(2)}) %all-to-all-start.5) | async-done | bytes 4194336 | tf_op jit(solution)/shard_map/all_to_all | solution.py:324
  494.7 8.5 %first_back.2 = (bf16[64,256,128]{2,1,0:T(8,128)(2,1)}, f32[512,256]{1,0:T(8,128)}) custom-call(bf16[256,64,128]{2,1,0:T(8,128)(2,1)} %bitcast.13.d, bf16[64,512,128]{2,1,0:T(8,128)(2,1)} %get-tuple-element.31.refs_0_.val), custom_call_target="tpu_custom_call" | custom-call | flops 2147483648 | bytes 16777216 | tf_op jit(solution)/shard_map/first_back/pallas_call | solution.py:233
  504.4 16.0 %grad_tokens.1 = (bf16[64,512,128]{2,1,0:T(8,128)(2,1)}, f32[128,128]{1,0:T(8,128)}) custom-call(bf16[64,256,128]{2,1,0:T(8,128)(2,1)} %get-tuple-element.38.refs_0_, bf16[64,256,128]{2,1,0:T(8,128)(2,1)} %get-tuple-element.41.refs_1_, bf16[64,512,128]{2,1,0:T(8,128)(2,1)} %get-tuple-element.42.refs_2_, bf16[64,512,128]{2,1,0:T(8,128)(2,1)} %bitcast.25, ...), custom_call_target="tpu_custom_call" | custom-call | flops 6442450944 | bytes 33554432 | tf_op jit(solution)/shard_map/grad_tokens/pallas_call | solution.py:274
  521.3 12.6 %all_to_all.56 = bf16[8,272,128]{2,1,0:T(8,128)(2,1)S(1)} all-to-all(bf16[8,272,128]{2,1,0:T(8,128)(2,1)S(1)} %bitcast.36), channel_id=1, replica_groups=mesh['dp'=4,'ctx'=8] {'ctx'}, dimensions={0} | all-to-all | bytes 1114112 | tf_op jit(solution)/shard_map/all_to_all | solution.py:293
  534.7 5.7 all-to-all-start.9
  540.4 52.0 %all-reduce.3.cloned.1.call-done = (f32[128,128]{1,0:T(8,128)}, f32[512,512]{1,0:T(8,128)}, f32[128,256]{1,0:T(8,128)}, f32[256,128]{1,0:T(8,128)}) async-done(((f32[128,128]{1,0:T(8,128)}, f32[512,512]{1,0:T(8,128)}, f32[128,256]{1,0:T(8,128)}, f32[256,128]{1,0:T(8,128)}), (f32[128,128]{1,0:T(8,128)}, f32[512,512]{1,0:T(8,128)}, f32[128,256]{1,0:T(8,128)}, ...) | async-done | bytes 1376272 | tf_op jit(solution)/shard_map/psum | solution.py:363
  594.9 3.5 all-to-all-start.10
  600.0 2.3 broadcast_multiply_fusion
  602.3 6.2 all-to-all-done.10
  (63 shorter events, 19.7 us)
Async XLA Ops:
  8.6 180.9 %copy-start.4 = (bf16[128,128]{1,0:T(8,128)(2,1)}, bf16[128,128]{1,0:T(8,128)(2,1)S(1)}, u32[]{:S(2)}) copy-start(bf16[128,128]{1,0:T(8,128)(2,1)S(1)} %get-tuple-element.65.wg) | copy-start | bytes 98308
  21.5 54.4 %all-to-all-start.2 = ((bf16[8,32,64,128]{3,2,1,0:T(8,128)(2,1)}), bf16[8,32,64,128]{3,2,1,0:T(8,128)(2,1)}, u32[]{:S(2)}, u32[]{:S(2)}) async-start(bf16[8,32,64,128]{3,2,1,0:T(8,128)(2,1)} %bitcast.34), calls=%async_computation.2 | async-start | bytes 8388608 | tf_op jit(solution)/shard_map/all_to_all | solution.py:324
  75.9 4.7 copy-start.3
  75.9 53.8 %all-to-all-start = ((bf16[8,32,64,128]{3,2,1,0:T(8,128)(2,1)}), bf16[8,32,64,128]{3,2,1,0:T(8,128)(2,1)}, u32[]{:S(2)}, u32[]{:S(2)}) async-start(bf16[8,32,64,128]{3,2,1,0:T(8,128)(2,1)} %bitcast.26), calls=%async_computation | async-start | bytes 8388608 | tf_op jit(solution)/shard_map/all_to_all | solution.py:324
  129.7 53.7 %all-to-all-start.3 = ((bf16[8,32,64,128]{3,2,1,0:T(8,128)(2,1)}), bf16[8,32,64,128]{3,2,1,0:T(8,128)(2,1)}, u32[]{:S(2)}, u32[]{:S(2)}) async-start(bf16[8,32,64,128]{3,2,1,0:T(8,128)(2,1)} %mix.3), calls=%async_computation.3 | async-start | bytes 8388608 | tf_op jit(solution)/shard_map/all_to_all | solution.py:324
  142.6 45.4 %copy-start.5 = (bf16[128,256]{1,0:T(8,128)(2,1)S(1)}, bf16[128,256]{1,0:T(8,128)(2,1)}, u32[]{:S(2)}) copy-start(bf16[128,256]{1,0:T(8,128)(2,1)} %wu.3) | copy-start | bytes 196612
  142.6 46.2 %copy-start.6 = (bf16[256,128]{1,0:T(8,128)(2,1)S(1)}, bf16[256,128]{1,0:T(8,128)(2,1)}, u32[]{:S(2)}) copy-start(bf16[256,128]{1,0:T(8,128)(2,1)} %wd.3) | copy-start | bytes 196612
  183.4 53.7 %all-to-all-start.1 = ((bf16[8,32,64,128]{3,2,1,0:T(8,128)(2,1)}), bf16[8,32,64,128]{3,2,1,0:T(8,128)(2,1)}, u32[]{:S(2)}, u32[]{:S(2)}) async-start(bf16[8,32,64,128]{3,2,1,0:T(8,128)(2,1)} %mix.2), calls=%async_computation.1 | async-start | bytes 8388608 | tf_op jit(solution)/shard_map/all_to_all | solution.py:324
  330.2 53.7 %all-to-all-start.4 = ((bf16[8,32,64,128]{3,2,1,0:T(8,128)(2,1)}), bf16[8,32,64,128]{3,2,1,0:T(8,128)(2,1)}, u32[]{:S(2)}, u32[]{:S(2)}) async-start(bf16[8,32,64,128]{3,2,1,0:T(8,128)(2,1)} %bitcast.32), calls=%async_computation.4 | async-start | bytes 8388608 | tf_op jit(solution)/shard_map/all_to_all | solution.py:324
  383.9 53.7 %all-to-all-start.7 = ((bf16[8,32,64,128]{3,2,1,0:T(8,128)(2,1)}), bf16[8,32,64,128]{3,2,1,0:T(8,128)(2,1)}, u32[]{:S(2)}, u32[]{:S(2)}) async-start(bf16[8,32,64,128]{3,2,1,0:T(8,128)(2,1)} %get-tuple-element.40), calls=%async_computation.7 | async-start | bytes 8388608 | tf_op jit(solution)/shard_map/all_to_all | solution.py:324
  437.6 5.2 copy-start.11
  437.6 5.9 copy-start.8
  437.6 5.9 copy-start.10
  437.6 6.6 %copy-start.7 = (f32[128,256]{1,0:T(8,128)S(1)}, f32[128,256]{1,0:T(8,128)}, u32[]{:S(2)}) copy-start(f32[128,256]{1,0:T(8,128)} %get-tuple-element.51) | copy-start | bytes 393220
  437.6 6.6 %copy-start.9 = (f32[128,256]{1,0:T(8,128)S(1)}, f32[128,256]{1,0:T(8,128)}, u32[]{:S(2)}) copy-start(f32[128,256]{1,0:T(8,128)} %get-tuple-element.52) | copy-start | bytes 393220
  437.6 7.2 %copy-start.12 = (f32[128,128]{1,0:T(8,128)S(1)}, f32[128,128]{1,0:T(8,128)}, u32[]{:S(2)}) copy-start(f32[128,128]{1,0:T(8,128)} %get-tuple-element.44) | copy-start | bytes 196612
  437.7 7.2 %copy-start.13 = (f32[128,128]{1,0:T(8,128)S(1)}, f32[128,128]{1,0:T(8,128)}, u32[]{:S(2)}) copy-start(f32[128,128]{1,0:T(8,128)} %get-tuple-element.45) | copy-start | bytes 196612
  437.7 7.9 %copy-start = (f32[512,512]{1,0:T(8,128)S(1)}, f32[512,512]{1,0:T(8,128)}, u32[]{:S(2)}) copy-start(f32[512,512]{1,0:T(8,128)} %get-tuple-element.50) | copy-start | bytes 3145732
  437.7 7.9 %copy-start.1 = (f32[512,512]{1,0:T(8,128)S(1)}, f32[512,512]{1,0:T(8,128)}, u32[]{:S(2)}) copy-start(f32[512,512]{1,0:T(8,128)} %get-tuple-element.49) | copy-start | bytes 3145732
  437.7 57.0 %all-to-all-start.5 = ((bf16[8,32,64,128]{3,2,1,0:T(8,128)(2,1)}), bf16[8,32,64,128]{3,2,1,0:T(8,128)(2,1)}, u32[]{:S(2)}, u32[]{:S(2)}) async-start(bf16[8,32,64,128]{3,2,1,0:T(8,128)(2,1)} %get-tuple-element.37), calls=%async_computation.5 | async-start | bytes 8388608 | tf_op jit(solution)/shard_map/all_to_all | solution.py:324
  442.6 149.8 %all-reduce.3.cloned.1.call-start = ((), (), s32[]{:S(2)}) async-start(), calls=%async_computation.11 | async-start | bytes 2752512 | tf_op jit(solution)/shard_map/psum | solution.py:363
  494.7 8.5 %copy-start.2 = (f32[512,256]{1,0:T(8,128)S(1)}, f32[512,256]{1,0:T(8,128)}, u32[]{:S(2)}) copy-start(f32[512,256]{1,0:T(8,128)} %get-tuple-element.47) | copy-start | bytes 1572868
  534.7 59.2 %all-to-all-start.9 = ((bf16[4,272,128]{2,1,0:T(8,128)(2,1)}), bf16[4,272,128]{2,1,0:T(8,128)(2,1)S(1)}, u32[]{:S(2)}, u32[]{:S(2)}) async-start(bf16[4,272,128]{2,1,0:T(8,128)(2,1)} %broadcast_in_dim.6), calls=%async_computation.9 | async-start | bytes 557056 | tf_op jit(solution)/shard_map/all_to_all | solution.py:293
  594.0 14.7 %copy-start.14 = (f32[128,128]{1,0:T(8,128)S(1)}, f32[128,128]{1,0:T(8,128)}, u32[]{:S(2)}) copy-start(f32[128,128]{1,0:T(8,128)} %get-tuple-element.55) | copy-start | bytes 196612
  594.9 13.6 %all-to-all-start.10 = ((bf16[8,272,128]{2,1,0:T(8,128)(2,1)}), bf16[8,272,128]{2,1,0:T(8,128)(2,1)S(1)}, u32[]{:S(2)}, u32[]{:S(2)}) async-start(bf16[8,272,128]{2,1,0:T(8,128)(2,1)} %broadcast_in_dim.7), calls=%async_computation.10 | async-start | bytes 1114112 | tf_op jit(solution)/shard_map/all_to_all | solution.py:293
Sparse Core Ops, SparseCore 0:
  449.8 142.5 all-reduce.2

commit v3 on v2

--- a/solution.py
+++ b/solution.py
@@ -212,7 +212,7 @@
         scratch_shapes=[pltpu.VMEM((TILE, per, width), F32)] * 2,
         input_output_aliases={9 + a: a for a in range(len(carried))},
         compiler_params=params(),
-        cost_estimate=cost(2 * rows * (6 * wu.size + 3 * wg.size), 12 * rows * width, rows * 3 * width),
+        cost_estimate=cost(10 * rows * (6 * wu.size + 3 * wg.size), 12 * rows * width, rows * 3 * width),
         name="mlp",
     )(tokens, cot, mix, *weights, *carried)
 
@@ -359,19 +359,23 @@
 
     axes = ("dp", "ctx")
     scale = float(seq_rows * n * lax.axis_size("dp")) ** (-0.5)
-    grad_second = sum(second)
-    grad_down, grad_up, grad_gate, grad_second = lax.psum(
-        (grad_down, grad_up, grad_gate, grad_second), axes
-    )
-    strips = [c[:, at : at + width] for c in first_cols for at in range(0, per, width)]
-    *strips, grad_value = summed_late([*strips, grad_value])
+    strips = [
+        wide[:, at : at + width]
+        for wide in (*first_cols, sum(second), grad_up)
+        for at in range(0, wide.shape[1], width)
+    ]
+    summed = summed_late([*strips, grad_down, grad_gate, grad_value])
+    grad_down, grad_gate, grad_value = summed[-3:]
+    count = steps // width
+    cols, cols_second, cols_up = summed[:count], summed[count:-3][: w_second.shape[1] // width], summed[:-3][-(w_up.shape[1] // width) :]
+    scale = float(seq_rows * n * lax.axis_size("dp")) ** (-0.5)
     return (
         carried[0].reshape(tokens.shape),
         grad_tokens.reshape(tokens.shape),
         jnp.concatenate([grad_gate, grad_value], axis=1) * scale,
-        jnp.concatenate(strips, axis=1) * scale,
-        grad_second * scale,
-        grad_up * scale,
+        jnp.concatenate(cols, axis=1) * scale,
+        jnp.concatenate(cols_second, axis=1) * scale,
+        jnp.concatenate(cols_up, axis=1) * scale,
         grad_down * scale,
     )
 

time: 619 us -> 580 us (0.937)
  waiting for transfers between devices: 304 us -> 246 us
  blocking collectives: 66.1 us -> 115 us
  between operations: 14.3 us -> 0.92 us
  starting transfers between devices: 42.5 us -> 33.1 us
  other arithmetic: 12.5 us -> 5.7 us
    psum x1 -> x0, waiting for transfers between devices: 52 us -> none  [body(): lax.psum((grad_down, grad_up, grad_gate, grad_second), axes)]
    all_to_all x1 -> x3, blocking collectives: 12.6 us -> 61.5 us  [swap(): return lax.all_to_all(a, axis, split_axis=0, concat_axis=0, tiled=True)]
    all_to_all x2 -> x0, starting transfers between devices: 9.21 us -> none  [swap(): return lax.all_to_all(a, axis, split_axis=0, concat_axis=0, tiled=True)]
  transfers between devices with their start and end apart: 10 -> 7, of which waited for: 9 -> 7; matrix products, arithmetic and copies ran while one was open for 2% -> 1% of each run, Pallas kernels for 19% -> 16%
where the time goes in v3:
time: 580 us; the launch traced here: 578 us
  waiting for transfers between devices  246 us (42%)
  Pallas kernels  168 us (29%)
  blocking collectives  115 us (20%)
  starting transfers between devices  33.1 us (6%)
  local copies, waits for them, and re-layouts  8.72 us (2%)
    all_to_all x7, waiting for transfers between devices, exchange(): lax.all_to_all(a.reshape(n, per // n, blocks, width), 'ctx', split_axis=0...  246 us
    pallas_call x2, Pallas kernels, mlp_call(): pl.pallas_call(mlp_kernel, grid=(blocks // TILE,), in_specs=[tile, tile,...  79.1 us
    all_to_all x3, blocking collectives, swap(): return lax.all_to_all(a, axis, split_axis=0, concat_axis=0, tiled=True)  61.5 us
    all_to_all x1, blocking collectives, exchange(): lax.all_to_all(a.reshape(n, per // n, blocks, width), 'ctx', split_axis=0...  53.6 us
    all_to_all x7, starting transfers between devices, exchange(): lax.all_to_all(a.reshape(n, per // n, blocks, width), 'ctx', split_axis=0...  33.1 us
    pallas_call x2, Pallas kernels, mix_back_call(): pl.pallas_call(mix_back_kernel, grid=(per // count,), in_specs=[spec, spe...  21.4 us
    pallas_call x2, Pallas kernels, back_call(): pl.pallas_call(back_kernel, grid=(blocks // TILE,), in_specs=[pl.BlockSpe...  16.9 us
    pallas_call x2, Pallas kernels, mix_call(): pl.pallas_call(mix_kernel, grid=(per // count,), in_specs=[spec, whole(w)...  16.4 us
  transfers between devices with their start and end apart: 7, of which 7 were waited for; matrix products, arithmetic and copies ran while one was open for 1% of the time, Pallas kernels for 16%

profile of v3, /device:TPU:0, one launch (start us, length us, event | category | flops | bytes accessed | tf_op | source)
XLA Modules:
  0.0 577.7 jit_solution(14651537843322349217)
XLA Ops:
  0.6 1.4 fusion.5
  2.0 1.3 copy.26
  4.1 10.8 %values_first.1 = (bf16[64,512,128]{2,1,0:T(8,128)(2,1)}, bf16[256,64,128]{2,1,0:T(8,128)(2,1)}) custom-call(bf16[64,512,128]{2,1,0:T(8,128)(2,1)} %bitcast.23, bf16[128,128]{1,0:T(8,128)(2,1)} %get-tuple-element.70.refs_1_, bf16[256,512]{1,0:T(8,128)(2,1)} %get-tuple-element.68.refs_2_), custom_call_target="tpu_custom_call" | custom-call | flops 3221225472 | bytes 20971520 | tf_op jit(solution)/shard_map/values_first/pallas_call | solution.py:73
  14.9 5.2 all-to-all-start.2
  20.1 7.6 %first_rest.1 = bf16[256,64,128]{2,1,0:T(8,128)(2,1)} custom-call(bf16[64,512,128]{2,1,0:T(8,128)(2,1)} %get-tuple-element.31.refs_0_.val, bf16[256,512]{1,0:T(8,128)(2,1)} %get-tuple-element.67.refs_1_), custom_call_target="tpu_custom_call" | custom-call | flops 2147483648 | bytes 12582912 | tf_op jit(solution)/shard_map/first_rest/pallas_call | solution.py:83
  27.7 41.7 %all-to-all-done.2.x = bf16[8,32,64,128]{3,2,1,0:T(8,128)(2,1)} async-done(((bf16[8,32,64,128]{3,2,1,0:T(8,128)(2,1)}), bf16[8,32,64,128]{3,2,1,0:T(8,128)(2,1)}, u32[]{:S(2)}, u32[]{:S(2)}) %all-to-all-start.2) | async-done | bytes 4194336 | tf_op jit(solution)/shard_map/all_to_all | solution.py:324
  69.3 4.7 all-to-all-start
  75.1 8.2 %mix.3 = bf16[8,32,64,128]{3,2,1,0:T(8,128)(2,1)} custom-call(bf16[8,32,64,128]{3,2,1,0:T(8,128)(2,1)} %all-to-all-done.2.x, bf16[512,512]{1,0:T(8,128)(2,1)} %bitcast.27), custom_call_target="tpu_custom_call" | custom-call | flops 2147483648 | bytes 8388608 | tf_op jit(solution)/shard_map/mix/pallas_call | solution.py:126
  83.2 39.9 %all-to-all-done.x = bf16[8,32,64,128]{3,2,1,0:T(8,128)(2,1)} async-done(((bf16[8,32,64,128]{3,2,1,0:T(8,128)(2,1)}), bf16[8,32,64,128]{3,2,1,0:T(8,128)(2,1)}, u32[]{:S(2)}, u32[]{:S(2)}) %all-to-all-start) | async-done | bytes 4194336 | tf_op jit(solution)/shard_map/all_to_all | solution.py:324
  123.2 4.6 all-to-all-start.3
  130.0 8.2 %mix.2 = bf16[8,32,64,128]{3,2,1,0:T(8,128)(2,1)} custom-call(bf16[8,32,64,128]{3,2,1,0:T(8,128)(2,1)} %all-to-all-done.x, bf16[512,512]{1,0:T(8,128)(2,1)} %bitcast.28), custom_call_target="tpu_custom_call" | custom-call | flops 2147483648 | bytes 8388608 | tf_op jit(solution)/shard_map/mix/pallas_call | solution.py:126
  138.2 38.7 %all-to-all-done.3 = bf16[8,32,64,128]{3,2,1,0:T(8,128)(2,1)} async-done(((bf16[8,32,64,128]{3,2,1,0:T(8,128)(2,1)}), bf16[8,32,64,128]{3,2,1,0:T(8,128)(2,1)}, u32[]{:S(2)}, u32[]{:S(2)}) %all-to-all-start.3) | async-done | bytes 4194336 | tf_op jit(solution)/shard_map/all_to_all | solution.py:324
  176.9 4.6 all-to-all-start.1
  181.5 39.5 %mlp.2 = (bf16[64,512,128]{2,1,0:T(8,128)(2,1)}, bf16[64,512,128]{2,1,0:T(8,128)(2,1)}, bf16[256,64,128]{2,1,0:T(8,128)(2,1)}, f32[256,128]{1,0:T(8,128)}, f32[128,256]{1,0:T(8,128)}, /*index=5*/f32[128,128]{1,0:T(8,128)}) custom-call(bf16[64,512,128]{2,1,0:T(8,128)(2,1)} %bitcast.24, bf16[64,512,128]{2,1,0:T(8,128)(2,1)} %bitcast.41, ...), custom_call_target="tpu_custom_call" | custom-call | flops 40265318400 | bytes 25165824 | tf_op jit(solution)/shard_map/mlp/pallas_call | solution.py:205
  221.0 9.6 %all-to-all-done.1 = bf16[8,32,64,128]{3,2,1,0:T(8,128)(2,1)} async-done(((bf16[8,32,64,128]{3,2,1,0:T(8,128)(2,1)}), bf16[8,32,64,128]{3,2,1,0:T(8,128)(2,1)}, u32[]{:S(2)}, u32[]{:S(2)}) %all-to-all-start.1) | async-done | bytes 4194336 | tf_op jit(solution)/shard_map/all_to_all | solution.py:324
  230.6 39.5 %mlp.3 = (bf16[64,512,128]{2,1,0:T(8,128)(2,1)}, bf16[64,512,128]{2,1,0:T(8,128)(2,1)}, bf16[256,64,128]{2,1,0:T(8,128)(2,1)}, f32[256,128]{1,0:T(8,128)}, f32[128,256]{1,0:T(8,128)}, /*index=5*/f32[128,128]{1,0:T(8,128)}) custom-call(bf16[64,512,128]{2,1,0:T(8,128)(2,1)} %bitcast.25, ...), custom_call_target="tpu_custom_call", output_to_operand_aliasing={{0}: (9, {}), {1}: (10, {})} | custom-call | flops 40265318400 | bytes 25165824 | tf_op jit(solution)/shard_map/mlp/pallas_call | solution.py:205
  270.1 53.6 %all_to_all.55.d = bf16[8,32,64,128]{3,2,1,0:T(8,128)(2,1)} all-to-all(bf16[8,32,64,128]{3,2,1,0:T(8,128)(2,1)} %bitcast.30), channel_id=1, replica_groups=mesh['dp'=4,'ctx'=8] {'ctx'}, dimensions={0} | all-to-all | bytes 8388608 | tf_op jit(solution)/shard_map/all_to_all | solution.py:324
  323.7 4.6 all-to-all-start.4
  328.3 10.7 %mix_back.3 = (bf16[8,32,64,128]{3,2,1,0:T(8,128)(2,1)}, f32[512,512]{1,0:T(8,128)}) custom-call(bf16[8,32,64,128]{3,2,1,0:T(8,128)(2,1)} %all-to-all-done.x, bf16[8,32,64,128]{3,2,1,0:T(8,128)(2,1)} %all_to_all.55.d, bf16[512,512]{1,0:T(8,128)(2,1)} %w.3), custom_call_target="tpu_custom_call" | custom-call | flops 4294967296 | bytes 12582912 | tf_op jit(solution)/shard_map/mix_back/pallas_call | solution.py:142
  339.0 38.4 %all-to-all-done.4.d = bf16[8,32,64,128]{3,2,1,0:T(8,128)(2,1)} async-done(((bf16[8,32,64,128]{3,2,1,0:T(8,128)(2,1)}), bf16[8,32,64,128]{3,2,1,0:T(8,128)(2,1)}, u32[]{:S(2)}, u32[]{:S(2)}) %all-to-all-start.4) | async-done | bytes 4194336 | tf_op jit(solution)/shard_map/all_to_all | solution.py:324
  377.4 4.6 all-to-all-start.7
  382.0 10.7 %mix_back.2 = (bf16[8,32,64,128]{3,2,1,0:T(8,128)(2,1)}, f32[512,512]{1,0:T(8,128)}) custom-call(bf16[8,32,64,128]{3,2,1,0:T(8,128)(2,1)} %all-to-all-done.2.x, bf16[8,32,64,128]{3,2,1,0:T(8,128)(2,1)} %all-to-all-done.4.d, bf16[512,512]{1,0:T(8,128)(2,1)} %w.3), custom_call_target="tpu_custom_call" | custom-call | flops 4294967296 | bytes 12582912 | tf_op jit(solution)/shard_map/mix_back/pallas_call | solution.py:142
  392.7 38.4 %all-to-all-done.7 = bf16[8,32,64,128]{3,2,1,0:T(8,128)(2,1)} async-done(((bf16[8,32,64,128]{3,2,1,0:T(8,128)(2,1)}), bf16[8,32,64,128]{3,2,1,0:T(8,128)(2,1)}, u32[]{:S(2)}, u32[]{:S(2)}) %all-to-all-start.7) | async-done | bytes 4194336 | tf_op jit(solution)/shard_map/all_to_all | solution.py:324
  431.2 4.9 all-to-all-start.5
  437.1 8.4 %first_back.3 = (bf16[64,256,128]{2,1,0:T(8,128)(2,1)}, f32[512,256]{1,0:T(8,128)}) custom-call(bf16[256,64,128]{2,1,0:T(8,128)(2,1)} %bitcast.15.d, bf16[64,512,128]{2,1,0:T(8,128)(2,1)} %get-tuple-element.31.refs_0_.val), custom_call_target="tpu_custom_call" | custom-call | flops 2147483648 | bytes 16777216 | tf_op jit(solution)/shard_map/first_back/pallas_call | solution.py:233
  445.5 39.5 %all-to-all-done.5 = bf16[8,32,64,128]{3,2,1,0:T(8,128)(2,1)} async-done(((bf16[8,32,64,128]{3,2,1,0:T(8,128)(2,1)}), bf16[8,32,64,128]{3,2,1,0:T(8,128)(2,1)}, u32[]{:S(2)}, u32[]{:S(2)}) %all-to-all-start.5) | async-done | bytes 4194336 | tf_op jit(solution)/shard_map/all_to_all | solution.py:324
  485.0 8.5 %first_back.2 = (bf16[64,256,128]{2,1,0:T(8,128)(2,1)}, f32[512,256]{1,0:T(8,128)}) custom-call(bf16[256,64,128]{2,1,0:T(8,128)(2,1)} %bitcast.13.d, bf16[64,512,128]{2,1,0:T(8,128)(2,1)} %get-tuple-element.31.refs_0_.val), custom_call_target="tpu_custom_call" | custom-call | flops 2147483648 | bytes 16777216 | tf_op jit(solution)/shard_map/first_back/pallas_call | solution.py:233
  495.6 15.9 %grad_tokens.1 = (bf16[64,512,128]{2,1,0:T(8,128)(2,1)}, f32[128,128]{1,0:T(8,128)}) custom-call(bf16[64,256,128]{2,1,0:T(8,128)(2,1)} %get-tuple-element.38.refs_0_, bf16[64,256,128]{2,1,0:T(8,128)(2,1)} %get-tuple-element.41.refs_1_, bf16[64,512,128]{2,1,0:T(8,128)(2,1)} %get-tuple-element.42.refs_2_, bf16[64,512,128]{2,1,0:T(8,128)(2,1)} %bitcast.26, ...), custom_call_target="tpu_custom_call" | custom-call | flops 6442450944 | bytes 33554432 | tf_op jit(solution)/shard_map/grad_tokens/pallas_call | solution.py:274
  512.3 19.9 %all_to_all.56 = bf16[8,608,128]{2,1,0:T(8,128)(2,1)S(1)} all-to-all(bf16[8,608,128]{2,1,0:T(8,128)(2,1)S(1)} %bitcast.33), channel_id=1, replica_groups=mesh['dp'=4,'ctx'=8] {'ctx'}, dimensions={0} | all-to-all | bytes 2490368 | tf_op jit(solution)/shard_map/all_to_all | solution.py:293
  532.5 21.7 %all_to_all.57 = bf16[4,608,128]{2,1,0:T(8,128)(2,1)S(1)} all-to-all(bf16[4,608,128]{2,1,0:T(8,128)(2,1)S(1)} %broadcast_in_dim.6), channel_id=1, replica_groups=mesh['dp'=4,'ctx'=8] {'dp'}, dimensions={0} | all-to-all | bytes 1245184 | tf_op jit(solution)/shard_map/all_to_all | solution.py:293
  554.5 19.9 %all_to_all.58 = bf16[8,608,128]{2,1,0:T(8,128)(2,1)S(1)} all-to-all(bf16[8,608,128]{2,1,0:T(8,128)(2,1)S(1)} %broadcast_in_dim.7), channel_id=1, replica_groups=mesh['dp'=4,'ctx'=8] {'ctx'}, dimensions={0} | all-to-all | bytes 2490368 | tf_op jit(solution)/shard_map/all_to_all | solution.py:293
  576.2 1.5 maximum_multiply_fusion
  (60 shorter events, 10.2 us)
Async XLA Ops:
  2.0 127.2 %copy-start.9 = (bf16[128,128]{1,0:T(8,128)(2,1)}, bf16[128,128]{1,0:T(8,128)(2,1)S(1)}, u32[]{:S(2)}) copy-start(bf16[128,128]{1,0:T(8,128)(2,1)S(1)} %get-tuple-element.69.wg) | copy-start | bytes 98308
  14.9 54.4 %all-to-all-start.2 = ((bf16[8,32,64,128]{3,2,1,0:T(8,128)(2,1)}), bf16[8,32,64,128]{3,2,1,0:T(8,128)(2,1)}, u32[]{:S(2)}, u32[]{:S(2)}) async-start(bf16[8,32,64,128]{3,2,1,0:T(8,128)(2,1)} %bitcast.31), calls=%async_computation.2 | async-start | bytes 8388608 | tf_op jit(solution)/shard_map/all_to_all | solution.py:324
  69.3 4.7 copy-start.3
  69.3 53.8 %all-to-all-start = ((bf16[8,32,64,128]{3,2,1,0:T(8,128)(2,1)}), bf16[8,32,64,128]{3,2,1,0:T(8,128)(2,1)}, u32[]{:S(2)}, u32[]{:S(2)}) async-start(bf16[8,32,64,128]{3,2,1,0:T(8,128)(2,1)} %bitcast.22), calls=%async_computation | async-start | bytes 8388608 | tf_op jit(solution)/shard_map/all_to_all | solution.py:324
  83.2 44.5 %copy-start.10 = (bf16[128,256]{1,0:T(8,128)(2,1)S(1)}, bf16[128,256]{1,0:T(8,128)(2,1)}, u32[]{:S(2)}) copy-start(bf16[128,256]{1,0:T(8,128)(2,1)} %wu.3) | copy-start | bytes 196612
  83.2 45.3 %copy-start.11 = (bf16[256,128]{1,0:T(8,128)(2,1)S(1)}, bf16[256,128]{1,0:T(8,128)(2,1)}, u32[]{:S(2)}) copy-start(bf16[256,128]{1,0:T(8,128)(2,1)} %wd.3) | copy-start | bytes 196612
  123.2 53.7 %all-to-all-start.3 = ((bf16[8,32,64,128]{3,2,1,0:T(8,128)(2,1)}), bf16[8,32,64,128]{3,2,1,0:T(8,128)(2,1)}, u32[]{:S(2)}, u32[]{:S(2)}) async-start(bf16[8,32,64,128]{3,2,1,0:T(8,128)(2,1)} %mix.3), calls=%async_computation.3 | async-start | bytes 8388608 | tf_op jit(solution)/shard_map/all_to_all | solution.py:324
  176.9 53.7 %all-to-all-start.1 = ((bf16[8,32,64,128]{3,2,1,0:T(8,128)(2,1)}), bf16[8,32,64,128]{3,2,1,0:T(8,128)(2,1)}, u32[]{:S(2)}, u32[]{:S(2)}) async-start(bf16[8,32,64,128]{3,2,1,0:T(8,128)(2,1)} %mix.2), calls=%async_computation.1 | async-start | bytes 8388608 | tf_op jit(solution)/shard_map/all_to_all | solution.py:324
  323.7 53.7 %all-to-all-start.4 = ((bf16[8,32,64,128]{3,2,1,0:T(8,128)(2,1)}), bf16[8,32,64,128]{3,2,1,0:T(8,128)(2,1)}, u32[]{:S(2)}, u32[]{:S(2)}) async-start(bf16[8,32,64,128]{3,2,1,0:T(8,128)(2,1)} %bitcast.29), calls=%async_computation.4 | async-start | bytes 8388608 | tf_op jit(solution)/shard_map/all_to_all | solution.py:324
  377.4 53.7 %all-to-all-start.7 = ((bf16[8,32,64,128]{3,2,1,0:T(8,128)(2,1)}), bf16[8,32,64,128]{3,2,1,0:T(8,128)(2,1)}, u32[]{:S(2)}, u32[]{:S(2)}) async-start(bf16[8,32,64,128]{3,2,1,0:T(8,128)(2,1)} %get-tuple-element.40), calls=%async_computation.7 | async-start | bytes 8388608 | tf_op jit(solution)/shard_map/all_to_all | solution.py:324
  431.1 4.9 copy-start.8
  431.1 5.7 copy-start.6
  431.2 5.7 copy-start.7
  431.2 5.7 copy-start
  431.2 5.7 copy-start.1
  431.2 53.8 %all-to-all-start.5 = ((bf16[8,32,64,128]{3,2,1,0:T(8,128)(2,1)}), bf16[8,32,64,128]{3,2,1,0:T(8,128)(2,1)}, u32[]{:S(2)}, u32[]{:S(2)}) async-start(bf16[8,32,64,128]{3,2,1,0:T(8,128)(2,1)} %get-tuple-element.37), calls=%async_computation.5 | async-start | bytes 8388608 | tf_op jit(solution)/shard_map/all_to_all | solution.py:324
  485.0 8.5 %copy-start.2 = (f32[512,256]{1,0:T(8,128)S(1)}, f32[512,256]{1,0:T(8,128)}, u32[]{:S(2)}) copy-start(f32[512,256]{1,0:T(8,128)} %get-tuple-element.45) | copy-start | bytes 1572868
  494.6 0.9 copy-start.4
  494.6 1.0 copy-start.5
  494.6 1.0 copy-start.12
  494.6 1.0 copy-start.13
